TPU v7x, 512 devices: a whole 4x8x8 slice. The times are simulated.
512 devices in a mesh: seq: 128 (over y, z, core), ch: 4 (over x).
Axes of the slice: x: 4, y: 8, z: 8, core: 2. Of those that a mesh axis runs over, the one named last changes fastest.
Arguments:
- features: bfloat16 [3, 32768, 4096], P(None, 'seq', 'ch'), may hold values from -6 to 6
- short_filter: bfloat16 [3, 7, 4096], P(None, None, 'ch'), may hold values from -2 to 2
- long_filter: bfloat16 [256, 128], replicated, may hold values from -0.5 to 0.5
- grad_out: bfloat16 [32768, 4096], P('seq', 'ch'), may hold values from -6 to 6
Outputs:
- grad_features: bfloat16 [3, 32768, 4096], P(None, 'seq', 'ch')
- grad_short: float32 [3, 7, 4096], P(None, None, 'ch')
- grad_long: float32 [256, 128], replicated
All inputs are finite; a program needn't handle non-finite values.
Results may differ from a plain program's by a relative error of at most 0.0073.
Values may be sent and summed in bfloat16 or wider, within the bound.
A program may use at most 64 MiB of HBM per device.

v0:
```python
import math

import jax
import jax.numpy as jnp
from jax import lax
from jax.sharding import PartitionSpec as P


def from_behind(value, axis, steps):
    count = lax.axis_size(axis)
    initial, last = (max(0, -steps), min(count, count - steps))
    return lax.ppermute(value, axis, [(source, source + steps) for source in range(initial, last)])


def slide_conv(signal, kernel):
    result = lax.conv_general_dilated(
        signal[None],
        kernel[:, None, :],
        (1,),
        "VALID",
        dimension_numbers=("NHC", "HIO", "NHC"),
        feature_group_count=signal.shape[-1],
        preferred_element_type=jnp.float32,
    )
    return result[0]


def body(features, short_filter, long_filter, grad_out):
    short_len = short_filter.shape[1]
    long_len = long_filter.shape[1]
    group_count = long_filter.shape[0]
    chan_width = features.shape[2]
    tok_rows = features.shape[1]
    long_taps = jnp.tile(long_filter.T, (1, chan_width // group_count))
    flipped = short_filter[:, ::-1, :]
    prior_rows = from_behind(features[:, tok_rows - (short_len - 1) :, :], "seq", 1)
    pre_ext = jnp.concatenate([prior_rows, features], axis=1)
    featured = jax.vmap(slide_conv)(pre_ext, flipped).astype(jnp.bfloat16)
    product = (featured[1].astype(jnp.float32) * featured[2].astype(jnp.float32)).astype(
        jnp.bfloat16
    )
    product_prior = from_behind(product[tok_rows - (long_len - 1) :], "seq", 1)
    product_ext = jnp.concatenate([product_prior, product], axis=0)
    query_feat = featured[0].astype(jnp.float32)
    key_feat = featured[1].astype(jnp.float32)
    value_feat = featured[2].astype(jnp.float32)
    filtered = slide_conv(product_ext, long_taps[::-1])
    grad_y = grad_out.astype(jnp.float32)
    grad_filtered = (grad_y * query_feat).astype(jnp.bfloat16)
    zero_rows = jnp.zeros((long_len - 1, chan_width), jnp.bfloat16)
    partial_all = slide_conv(
        jnp.concatenate([zero_rows, grad_filtered, zero_rows], axis=0), long_taps
    )
    edge_part = from_behind(partial_all[: long_len - 1], "seq", -1)
    head_zeros = jnp.zeros((tok_rows - (long_len - 1), chan_width), jnp.float32)
    grad_product = partial_all[long_len - 1 :] + jnp.concatenate([head_zeros, edge_part], axis=0)
    grad_featured = jnp.stack(
        [grad_y * filtered, grad_product * value_feat, grad_product * key_feat]
    ).astype(jnp.bfloat16)
    later_grads = from_behind(grad_featured[:, : short_len - 1, :], "seq", -1)
    grad_ext = jnp.concatenate([grad_featured, later_grads], axis=1)
    grad_features = jax.vmap(slide_conv)(grad_ext, short_filter).astype(jnp.bfloat16)
    short_terms = jax.vmap(slide_conv)(pre_ext, grad_featured)[:, ::-1, :]
    long_channel = slide_conv(product_ext, grad_filtered)[::-1]
    long_terms = (
        long_channel.reshape(long_len, chan_width // group_count, group_count).sum(axis=1).T
    )
    token_count = tok_rows * lax.axis_size("seq")
    short_total = lax.psum(short_terms, "seq")
    long_total = lax.psum(long_terms, ("seq", "ch"))
    grad_short = short_total / math.sqrt(token_count)
    grad_long = (
        long_total
        / math.sqrt(
            token_count * group_count * 0
            + token_count * (chan_width * lax.axis_size("ch") // group_count)
        )
        * 1.0
    )
    return (grad_features, grad_short, grad_long)


def solution(mesh):
    in_specs = (P(None, "seq", "ch"), P(None, None, "ch"), P(), P("seq", "ch"))
    out_specs = (P(None, "seq", "ch"), P(None, None, "ch"), P())
    return jax.shard_map(body, mesh=mesh, in_specs=in_specs, out_specs=out_specs, check_vma=False)
```

profile of v0, /device:TPU:1, one launch (start us, length us, event | category | flops | bytes accessed | tf_op | source)
XLA Modules:
  0.0 579.4 jit_solution(6045019349113524694)
XLA Ops:
  9.0 5.4 collective-permute-start
  14.4 2.9 rev.12
  18.3 2.6 rev.13
  23.9 3.3 reshape.123
  27.2 2.7 pad.1
  30.0 2.0 reshape.136
  32.9 2.0 fusion.3
  40.6 1.8 fusion.30
  42.5 2.2 collective-permute-start.1
  45.0 23.3 %fusion.6 = f32[1,383,1024]{2,0,1:T(1,128)S(1)} fusion(bf16[128,1,1024]{2,1,0:T(2,128)(2,1)S(1)} %copy-done.6, bf16[1,510,1024]{2,1,0:T(8,128)(2,1)S(1)} %maximum_bitcast_fusion.3), kind=kOutput, calls=%fused_computation.9 | convolution fusion | flops 100401152 | bytes 2875392 | tf_op jit(solution)/shard_map/conv_general_dilated | solution.py:16
  71.0 4.1 collective-permute-start.2
  75.2 13.9 %fusion.20 = f32[1,128,1024]{2,0,1:T(1,128)S(1)} fusion(bf16[1,383,1024]{2,1,0:T(8,128)(2,1)S(1)} %maximum_bitcast_fusion.4, bf16[256,1,1024]{2,0,1:T(8,128)(2,1)S(1)} %bitcast.109), kind=kOutput, calls=%fused_computation.29 | convolution fusion | flops 67108864 | bytes 1832960 | tf_op jit(solution)/shard_map/conv_general_dilated | solution.py:16
  89.1 14.8 %fusion.22 = f32[1,256,1024]{2,0,1:T(1,128)} fusion(bf16[1,383,1024]{2,1,0:T(8,128)(2,1)S(1)} %maximum_bitcast_fusion.4, bf16[128,1,1024]{2,0,1:T(8,128)(2,1)S(1)} %bitcast.113), kind=kOutput, calls=%fused_computation.31 | convolution fusion | flops 67108864 | bytes 2095104 | tf_op jit(solution)/shard_map/conv_general_dilated | solution.py:16
  105.6 2.3 fusion.45
  107.9 262.2 %all-reduce.6.cloned.1.call-done = f32[256,128]{0,1:T(8,128)} async-done(((f32[256,128]{0,1:T(8,128)}), f32[256,128]{0,1:T(8,128)}) %all-reduce.6.cloned.1.call-update) | async-done | bytes 131088 | tf_op jit(solution)/shard_map/psum | solution.py:70
  371.7 1.9 fusion.29
  373.7 2.1 collective-permute-start.3
  377.6 7.7 %copy.63 = bf16[256,1,3072]{2,1,0:T(2,128)(2,1)} copy(bf16[256,1,3072]{0,2,1:T(8,128)(2,1)} %bitcast.106) | data formatting | bytes 3145728 | tf_op jit(solution)/shard_map/vmap()/reshape | solution.py:16
  385.3 8.6 %fusion.24 = f32[7,3072]{1,0:T(8,128)S(1)} fusion(bf16[256,1,3072]{2,1,0:T(2,128)(2,1)} %copy.63, bf16[1,262,3072]{2,1,0:T(8,128)(2,1)S(1)} %copy-done.2), kind=kOutput, calls=%fused_computation.33 | convolution fusion | flops 11010048 | bytes 3268608 | tf_op jit(solution)/shard_map/vmap()/conv_general_dilated | solution.py:16
  396.3 3.3 reshape.127
  399.6 2.7 pad.3
  402.3 2.0 reshape.143
  405.3 2.0 fusion.2
  413.8 156.5 %all-reduce.4.cloned.1.call-done = f32[3,7,1024]{2,0,1:T(4,128)} async-done(((f32[3,7,1024]{2,0,1:T(4,128)}), f32[3,7,1024]{2,0,1:T(4,128)}) %all-reduce.4.cloned.1.call-update) | async-done | bytes 86032 | tf_op jit(solution)/shard_map/psum | solution.py:69
  (74 shorter events, 31.1 us)
Async XLA Ops:
  8.0 14.1 %copy-start.5 = (bf16[3,256,1024]{2,1,0:T(8,128)(2,1)S(1)}, bf16[3,256,1024]{2,1,0:T(8,128)(2,1)}, u32[]{:S(2)}) copy-start(bf16[3,256,1024]{2,1,0:T(8,128)(2,1)} %param.4) | copy-start | bytes 4718596
  8.0 362.1 %all-reduce.6.cloned.1.call-start = ((), (), s32[]{:S(2)}) async-start(), calls=%async_computation.1 | async-start | bytes 262144 | tf_op jit(solution)/shard_map/psum | solution.py:70
  9.0 13.1 %collective-permute-start = (bf16[3,6,1024]{2,1,0:T(8,128)(2,1)S(1)}, bf16[3,6,1024]{2,1,0:T(8,128)(2,1)S(1)}, u32[]{:S(2)}, u32[]{:S(2)}) collective-permute-start(bf16[3,6,1024]{2,1,0:T(8,128)(2,1)S(1)} %slice.35), channel_id=1, source_target_pairs={{0,4},{4,8},{8,12},{12,16},{16,20},{20,24},{24,28},{28,32},{32,36}... | collective-permute-start | bytes 110600 | tf_op jit(solution)/shard_map/ppermute | solution.py:12
  31.9 1.0 copy-start.9
  37.6 1.4 slice-start
  40.6 4.2 copy-start
  42.4 2.6 copy-start.6
  42.5 32.6 %collective-permute-start.1 = (bf16[127,1024]{1,0:T(8,128)(2,1)S(1)}, bf16[127,1024]{1,0:T(8,128)(2,1)S(1)}, u32[]{:S(2)}, u32[]{:S(2)}) collective-permute-start(bf16[127,1024]{1,0:T(8,128)(2,1)S(1)} %slice.53), channel_id=1, source_target_pairs={{0,4},{4,8},{8,12},{12,16},{16,20},{20,24},{24,28},{28,32},{32,36}... | collective-permute-start | bytes 780296 | tf_op jit(solution)/shard_map/ppermute | solution.py:12
  71.0 300.8 %collective-permute-start.2 = (f32[127,1024]{1,0:T(8,128)}, f32[127,1024]{1,0:T(8,128)}, u32[]{:S(2)}, u32[]{:S(2)}) collective-permute-start(f32[127,1024]{1,0:T(8,128)} %bitcast.94), channel_id=1, source_target_pairs={{4,0},{8,4},{12,8},{16,12},{20,16},{24,20},{28,24},{32,28},{36,32}... | collective-permute-start | bytes 1560584 | tf_op jit(solution)/shard_map/ppermute | solution.py:12
  75.2 13.9 %copy-start.7 = (bf16[128,1024]{1,0:T(8,128)(2,1)S(1)}, bf16[128,1024]{1,0:T(8,128)(2,1)}, u32[]{:S(2)}) copy-start(bf16[128,1024]{1,0:T(8,128)(2,1)} %rev.13) | copy-start | bytes 786436
  103.9 1.7 copy-start.3
  104.5 267.2 %copy-start.1 = (bf16[1,256,3,1024]{3,1,0,2:T(8,128)(2,1)S(1)}, bf16[1,256,3,1024]{3,1,0,2:T(8,128)(2,1)}, u32[]{:S(2)}) copy-start(bf16[1,256,3,1024]{3,1,0,2:T(8,128)(2,1)} %copy-done) | copy-start | bytes 4718596
  105.5 464.8 %all-reduce.4.cloned.1.call-start = ((), (), s32[]{:S(2)}) async-start(), calls=%async_computation | async-start | bytes 229376 | tf_op jit(solution)/shard_map/psum | solution.py:69
  371.7 4.1 copy-start.4
  373.7 21.0 %collective-permute-start.3 = (bf16[3,6,1024]{2,1,0:T(8,128)(2,1)S(1)}, bf16[3,6,1024]{2,1,0:T(8,128)(2,1)S(1)}, u32[]{:S(2)}, u32[]{:S(2)}) collective-permute-start(bf16[3,6,1024]{2,1,0:T(8,128)(2,1)S(1)} %pad_maximum_fusion), channel_id=1, source_target_pairs={{4,0},{8,4},{12,8},{16,12},{20,16},{24,20},{28,24},{32,28},{36,32}... | collective-permute-start | bytes 110600 | tf_op jit(solution)/shard_map/ppermute | solution.py:12
  377.6 7.7 %copy-start.2 = (bf16[1,262,3072]{2,1,0:T(8,128)(2,1)S(1)}, bf16[1,262,3072]{2,1,0:T(8,128)(2,1)}, u32[]{:S(2)}) copy-start(bf16[1,262,3072]{2,1,0:T(8,128)(2,1)} %reshape.123) | copy-start | bytes 4829188
  404.3 1.0 copy-start.8
  404.3 1.0 copy-start.10
  409.9 1.4 slice-start.1
Sparse Core Ops, SparseCore 0:
  105.6 264.3 all-reduce.5
Sparse Core Ops, SparseCore 1:
  394.8 175.5 all-reduce.3
where the time goes:
time: 580 us; the launch traced here: 579 us
  waiting for transfers between devices  419 us (72%)
  matrix products  64.6 us (11%)
  local copies, waits for them, and re-layouts  56.2 us (10%)
  between operations  15.9 us (3%)
  starting transfers between devices  13.9 us (2%)
  other arithmetic  10 us (2%)
    psum x1, waiting for transfers between devices, body(): long_total = lax.psum(long_terms, ('seq', 'ch'))  262 us
    psum x1, waiting for transfers between devices, body(): short_total = lax.psum(short_terms, 'seq')  157 us
    conv_general_dilated x6, matrix products, slide_conv(): lax.conv_general_dilated(signal[None], kernel[:, None, :], (1,), 'VALID',...  64.6 us
    reshape x9, local copies, waits for them, and re-layouts, slide_conv(): lax.conv_general_dilated(signal[None], kernel[:, None, :], (1,), 'VALID',...  24.1 us
    ppermute x4, starting transfers between devices, from_behind(): lax.ppermute(value, axis, [(source, source + steps) for source in range(i...  13.8 us
  transfers between devices with their start and end apart: 6, of which 2 were waited for; matrix products, arithmetic and copies ran while one was open for 18% of the time, Pallas kernels for 0%

commit v1 on v0

v1 whole, which is shorter than its diff:
```python
import functools
import math

import jax
import jax.numpy as jnp
import ml_dtypes
import numpy as np
from jax import lax
from jax.experimental import pallas as pl
from jax.experimental.pallas import tpu as pltpu
from jax.sharding import PartitionSpec as P

MESH = pl.DeviceIdType.MESH
BF = jnp.bfloat16
F32 = jnp.float32
ROWS = 256
TAPS = 128
SHORT = 7
GROUPS = 256
N = ROWS + TAPS
HALF = N // 2


def split(matrix):
    high = matrix.astype(ml_dtypes.bfloat16)
    low = (matrix - high.astype(np.float64)).astype(ml_dtypes.bfloat16)
    return high, low


def transforms():
    angle = 2 * np.pi * (np.arange(HALF) + 0.5) / N

    def rows(tokens):
        phase = np.outer(angle, tokens)
        return np.concatenate([np.cos(phase), -np.sin(phase)], axis=0)

    local = rows(np.arange(ROWS))
    behind = rows(np.arange(-TAPS, 0))
    forward = np.concatenate([*split(local), *split(behind)], axis=1)
    inverse = np.concatenate(split(local.T / HALF), axis=1)
    return forward, inverse


def kernel(
    dims,
    feat,
    short,
    long,
    gout,
    fwd,
    inv,
    out,
    gs_out,
    gl_out,
    fb,
    gob,
    fwdv,
    invv,
    shortv,
    longv,
    coef,
    xf,
    kb,
    vb,
    prod,
    gfil,
    xhalo,
    yhalo,
    fhalo,
    qhead,
    ghead,
    qn,
    hs,
    xs,
    ys,
    rs,
    rsplit,
    shi,
    slo,
    filt,
    gf,
    gsend,
    grecv,
    outv,
    glp,
    glrecv,
    glb,
    glex,
    glmid,
    glex2,
    glfin,
    gsp,
    gscore,
    gsb,
    gsex,
    gsmid,
    gsex2,
    gsfin,
    ld_sem,
    st_sem,
    halo_s,
    halo_r,
    gl_s,
    gl_r,
    gs_s,
    gs_r,
):
    n_seq, n_ch, n_y, n_z, lanes = dims
    tiles = lanes // 128
    chunks = lanes // 256
    halves = tiles // 4
    s = lax.axis_index("seq")
    ch = lax.axis_index("ch")
    core = lax.rem(s, 2)
    z = lax.rem(s // 2, n_z)
    y = s // (2 * n_z)

    def at(yy, zz, cc):
        return (yy * n_z + zz) * 2 + cc

    ahead = {"seq": lax.rem(s + 1, n_seq)}
    behind = {"seq": lax.rem(s + n_seq - 1, n_seq)}
    sibling = {"seq": at(y, z, 1 - core)}
    ys_peers = [{"seq": at(lax.rem(y + d, n_y), z, core)} for d in range(1, n_y)]
    zs_peers = [{"seq": at(y, lax.rem(z + d, n_z), core)} for d in range(1, n_z)]
    n_own = 2 * n_ch
    own = ch * 2 + core
    xc_peers = []
    for d in range(1, n_own):
        o = lax.rem(own + d, n_own)
        xc_peers.append(({"seq": at(y, z, lax.rem(o, 2)), "ch": o // 2}, o))

    barrier = pltpu.get_barrier_semaphore()
    greet = [ahead, behind] + ys_peers + zs_peers + [p for p, _ in xc_peers]
    for p in greet:
        pl.semaphore_signal(barrier, inc=1, device_id=p, device_id_type=MESH)

    def load(src, dst, i):
        c = pltpu.make_async_copy(src, dst, ld_sem.at[i])
        c.start()
        return c

    f_loads, g_loads = [], []
    c_short = load(short, shortv, 2 * tiles)
    for l in range(tiles):
        f_loads.append(load(feat.at[:, :, l * 128 : (l + 1) * 128], fb.at[l], l))
    for l in range(tiles):
        g_loads.append(load(gout.at[:, l * 128 : (l + 1) * 128], gob.at[l], tiles + l))
    c_long = load(long, longv, 2 * tiles + 1)
    c_fwd = load(fwd, fwdv, 2 * tiles + 2)
    c_inv = load(inv, invv, 2 * tiles + 3)

    def remote(src, dst, ssem, rsem, peer):
        c = pltpu.make_async_remote_copy(
            src_ref=src, dst_ref=dst, send_sem=ssem, recv_sem=rsem, device_id=peer, device_id_type=MESH
        )
        c.start()
        return c

    c_short.wait()
    for i in range(3):
        taps = shortv[i].astype(F32)
        for l in range(tiles):
            coef[l, i, 0:SHORT, :] = taps[:, l * 128 : (l + 1) * 128]
    for c in f_loads:
        c.wait()

    def tap(l, i):
        return [coef[l, i, j : j + 1, :] for j in range(SHORT)]

    def fir(ref, l, i, c, first):
        total = c[0] * ref[l, i, first : first + 16, :]
        for j in range(1, SHORT):
            total = total + c[j] * ref[l, i, first - j : first - j + 16, :]
        return total.astype(BF)

    def widen(l, i, lo, hi):
        for r in range(lo, hi, 16):
            xf[l, i, 8 + r : 24 + r, :] = fb[l, i, r : r + 16, :].astype(F32)

    def lane(l):
        return pl.ds(pl.multiple_of(lax.rem(l, 2) * 128, 128), 128)

    def product_rows(l, lo, hi):
        ck, cv = tap(l, 1), tap(l, 2)
        for r in range(lo, hi, 16):
            k = fir(xf, l, 1, ck, 8 + r)
            v = fir(xf, l, 2, cv, 8 + r)
            kb[l, r : r + 16, :] = k
            vb[l, r : r + 16, :] = v
            prod[l // 2, r : r + 16, lane(l)] = (k.astype(F32) * v.astype(F32)).astype(BF)

    def grad_rows(l, lo, hi):
        cq = tap(l, 0)
        for r in range(lo, hi, 16):
            q = fir(xf, l, 0, cq, 8 + r)
            gfil[l // 2, r : r + 16, lane(l)] = (
                q.astype(F32) * gob[l, r : r + 16, :].astype(F32)
            ).astype(BF)

    def tail(l, _):
        widen(l, 1, 112, ROWS)
        widen(l, 2, 112, ROWS)
        product_rows(l, 128, ROWS)
        return 0

    lax.fori_loop(0, tiles, tail, 0)

    pl.semaphore_wait(barrier, len(greet))
    sends = []
    c_fh = remote(feat.at[:, ROWS - 16 :, :], fhalo, halo_s.at[0], halo_r.at[0], ahead)
    c_qh = remote(feat.at[0, 0:16, :], qhead, halo_s.at[1], halo_r.at[1], behind)
    c_gh = remote(gout.at[0:16, :], ghead, halo_s.at[2], halo_r.at[2], behind)
    c_x, c_y, c_g = {}, {}, {}
    for q in range(chunks):
        c_x[q] = remote(
            prod.at[q, ROWS - TAPS :, :], xhalo.at[q], halo_s.at[3 + q], halo_r.at[3 + q], ahead
        )

    for c in g_loads:
        c.wait()

    def head(l, _):
        widen(l, 0, 0, 128)
        grad_rows(l, 16, 128)
        return 0

    order = list(range(chunks // 2, chunks)) + list(range(chunks // 2))
    for q in order:
        lax.fori_loop(2 * q, 2 * q + 2, head, 0)
        i = 3 + chunks + q
        c_y[q] = remote(
            gfil.at[q, 16:TAPS, :], yhalo.at[q, 16:TAPS, :], halo_s.at[i], halo_r.at[i], behind
        )

    def rest(l, _):
        widen(l, 0, 128, ROWS)
        grad_rows(l, 128, ROWS)
        widen(l, 1, 0, 112)
        widen(l, 2, 0, 112)
        product_rows(l, 16, 128)
        return 0

    lax.fori_loop(0, tiles, rest, 0)

    c_long.wait()
    c_fwd.wait()
    nt = (((1,), (1,)), ((), ()))
    hs[...] = lax.dot_general(fwdv[:, 0:TAPS], longv[...], nt, preferred_element_type=F32) + lax.dot_general(
        fwdv[:, ROWS : ROWS + TAPS], longv[...], nt, preferred_element_type=F32
    )

    not_first = jnp.where(s > 0, 1.0, 0.0).astype(F32)
    not_last = jnp.where(s < n_seq - 1, 1.0, 0.0).astype(F32)
    c_fh.wait()
    c_qh.wait()
    c_gh.wait()
    for l in range(tiles):
        cols = slice(l * 128, (l + 1) * 128)
        for i in range(3):
            xf[l, i, 0:8, :] = fhalo[i, :, cols].astype(F32)[8:16] * not_first
        qn[l, 0, 0:8, :] = xf[l, 0, ROWS : ROWS + 8, :]
        qn[l, 0, 8:24, :] = qhead[:, cols].astype(F32)
        product_rows(l, 0, 16)
        grad_rows(l, 0, 16)
        qq = fir(qn, l, 0, tap(l, 0), 8)
        yhalo[l // 2, 0:16, (l % 2) * 128 : (l % 2) * 128 + 128] = (
            qq.astype(F32) * ghead[:, cols].astype(F32)
        ).astype(BF)

    def dot(a, b):
        return jnp.dot(a, b, preferred_element_type=F32)

    def local(q, _):
        p = prod[q]
        xs[q] = dot(fwdv[:, 0:ROWS], p) + dot(fwdv[:, ROWS : 2 * ROWS], p)
        g = gfil[q]
        ys[q] = dot(fwdv[:, 0:ROWS], g) + dot(fwdv[:, ROWS : 2 * ROWS], g)
        return 0

    lax.fori_loop(0, chunks, local, 0)

    def far(h):
        return dot(fwdv[:, 2 * ROWS : 2 * ROWS + TAPS], h) + dot(fwdv[:, 2 * ROWS + TAPS :], h)

    def add_x(q):
        c_x[q].wait()
        xs[q] = xs[q] + not_first * far(xhalo[q])

    def add_y(q):
        c_y[q].wait()
        ys[q] = ys[q] - not_last * far(yhalo[q])

    def corr(q, first):
        def block(b, _):
            re = pl.ds(pl.multiple_of(b * 16, 16), 16)
            im = pl.ds(pl.multiple_of(b * 16 + HALF, 16), 16)
            xr, xi, yr, yi = xs[q, re, :], xs[q, im, :], ys[q, re, :], ys[q, im, :]
            rr = xr * yr + xi * yi
            ri = xr * yi - xi * yr
            if not first:
                rr = rr + rs[re, :]
                ri = ri + rs[im, :]
            rs[re, :] = rr
            rs[im, :] = ri
            return 0

        lax.fori_loop(0, HALF // 16, block, 0)

    def hilo(value):
        high = value.astype(BF)
        return high, (value - high.astype(F32)).astype(BF)

    for q in range(chunks // 2):
        add_x(q)
        corr(q, q == 0)
    for q in range(chunks // 2, chunks):
        add_y(q)
        corr(q, False)
    c_inv.wait()
    rh, rl = hilo(rs[...])
    glp[...] = (
        dot(invv[0:TAPS, 0:N], rh) + dot(invv[0:TAPS, N:], rh) + dot(invv[0:TAPS, 0:N], rl)
    )

    own_rows = TAPS // n_own
    mine = pl.ds(pl.multiple_of(own * own_rows, own_rows), own_rows)
    gl_c = []
    for d, (p, o) in enumerate(xc_peers):
        piece = pl.ds(pl.multiple_of(o * own_rows, own_rows), own_rows)
        gl_c.append(remote(glp.at[piece, :], glrecv.at[d], gl_s.at[0, 0, d], gl_r.at[0, 0, d], p))

    def spread(src, dst, sems, peers):
        ss, rr = sems
        return [remote(src, dst.at[d], ss.at[d], rr.at[d], p) for d, p in enumerate(peers)]

    def gl_one():
        for c in gl_c:
            c.wait()
        total = glp[mine, :]
        for d in range(n_own - 1):
            total = total + glrecv[d]
        res = []
        for k in range(2):
            glb[k] = total[:, k * 128 : (k + 1) * 128].astype(BF)
            peers = ys_peers if k == 0 else zs_peers
            res.append(spread(glb.at[k], glex.at[k], (gl_s.at[1, k], gl_r.at[1, k]), peers))
        return res

    def gl_two(cs):
        res = []
        for k in range(2):
            for c in cs[k]:
                c.wait()
            total = glb[k].astype(F32)
            for d in range(len(cs[k])):
                total = total + glex[k, d].astype(F32)
            glmid[k] = total.astype(BF)
            peers = zs_peers if k == 0 else ys_peers
            res.append(spread(glmid.at[k], glex2.at[k], (gl_s.at[2, k], gl_r.at[2, k]), peers))
        return res

    def gl_three(cs):
        for k in range(2):
            for c in cs[k]:
                c.wait()
            total = glmid[k].astype(F32)
            for d in range(len(cs[k])):
                total = total + glex2[k, d].astype(F32)
            glfin[mine, k * 128 : (k + 1) * 128] = total
        res = []
        for d, (p, _) in enumerate(xc_peers):
            res.append(remote(glfin.at[mine, :], glfin.at[mine, :], gl_s.at[3, 0, d], gl_r.at[3, 0, d], p))
        return res

    def gl_four(cs):
        for c in cs:
            c.wait()
        gl_out[...] = glfin[...].T

    def gs_zero(h):
        theirs = pl.ds(4 * h + 2 * (1 - core), 2)
        return remote(gsp.at[theirs], gscore.at[h], gs_s.at[h, 0, 0], gs_r.at[h, 0, 0], sibling)

    def gs_one(h, c):
        c.wait()
        total = gsp[pl.ds(4 * h + 2 * core, 2)] + gscore[h]
        gsb[h] = total.reshape(48, 128).astype(BF)
        peers = ys_peers if h % 2 == 0 else zs_peers
        return spread(gsb.at[h], gsex.at[h], (gs_s.at[h, 1], gs_r.at[h, 1]), peers)

    def gs_two(h, cs):
        for c in cs:
            c.wait()
        total = gsb[h].astype(F32)
        for d in range(len(cs)):
            total = total + gsex[h, d].astype(F32)
        gsmid[h] = total.astype(BF)
        peers = zs_peers if h % 2 == 0 else ys_peers
        return spread(gsmid.at[h], gsex2.at[h], (gs_s.at[h, 2], gs_r.at[h, 2]), peers)

    def gs_three(h, cs):
        for c in cs:
            c.wait()
        total = gsmid[h].astype(F32)
        for d in range(len(cs)):
            total = total + gsex2[h, d].astype(F32)
        here = pl.ds(4 * h + 2 * core, 2)
        gsfin[here] = total.reshape(2, 24, 128)
        return remote(gsfin.at[here], gsfin.at[here], gs_s.at[h, 3, 0], gs_r.at[h, 3, 0], sibling)

    def gs_four(h, c):
        c.wait()
        for l in range(4 * h, 4 * h + 4):
            for i in range(3):
                gs_out[i, :, l * 128 : (l + 1) * 128] = gsfin[l, 8 * i : 8 * i + 8, :]

    def spectra(q):
        def block(b, _):
            re = pl.ds(pl.multiple_of(b * 16, 16), 16)
            im = pl.ds(pl.multiple_of(b * 16 + HALF, 16), 16)
            hr, hi = hs[re, :], hs[im, :]
            xr, xi = xs[q, re, :], xs[q, im, :]
            yr, yi = ys[q, re, :], ys[q, im, :]
            parts = (
                (re, 0, xr * hr - xi * hi),
                (im, 0, xr * hi + xi * hr),
                (re, 256, yr * hr + yi * hi),
                (im, 256, yi * hr - yr * hi),
            )
            for rows, c, value in parts:
                high, low = hilo(value)
                shi[rows, c : c + 256] = high
                slo[rows, c : c + 256] = low
            return 0

        lax.fori_loop(0, HALF // 16, block, 0)
        for c in (0, 256):
            sh = shi[:, c : c + 256]
            filt[:, c : c + 256] = (
                dot(invv[:, 0:N], sh) + dot(invv[:, N:], sh) + dot(invv[:, 0:N], slo[:, c : c + 256])
            )

    def featured_grad(l, h):
        for r in range(0, ROWS, 16):
            rows = slice(r, r + 16)
            fa = filt[rows, h * 128 : h * 128 + 128]
            fg = filt[rows, 256 + h * 128 : 256 + h * 128 + 128]
            g0 = (gob[l, rows, :].astype(F32) * fa).astype(BF)
            g1 = (fg * vb[l, rows, :].astype(F32)).astype(BF)
            g2 = (fg * kb[l, rows, :].astype(F32)).astype(BF)
            for i, g in enumerate((g0, g1, g2)):
                gf[l, i, rows, :] = g.astype(F32)
                if r == 0:
                    gsend[l, i] = g

    def short_grad(l):
        for i in range(3):
            acc = [jnp.zeros((8, 128), F32) for _ in range(SHORT)]
            for r in range(0, ROWS, 8):
                g = gf[l, i, r : r + 8, :]
                for j in range(SHORT):
                    acc[j] = acc[j] + g * xf[l, i, 8 + r - j : 16 + r - j, :]
            rows = [jnp.sum(a, axis=0, keepdims=True) for a in acc]
            rows.append(jnp.zeros((1, 128), F32))
            gsp[l, 8 * i : 8 * i + 8, :] = jnp.concatenate(rows, axis=0)

    def chunk(q):
        if q < chunks // 2:
            add_y(q)
        else:
            add_x(q)
        spectra(q)
        for h in range(2):
            featured_grad(2 * q + h, h)
        i = 3 + 2 * chunks + q
        two = pl.ds(2 * q, 2)
        c_g[q] = remote(gsend.at[two], grecv.at[two], halo_s.at[i], halo_r.at[i], behind)

        def sg(l, _):
            short_grad(l)
            return 0

        lax.fori_loop(2 * q, 2 * q + 2, sg, 0)

    def conv(q):
        c_g[q].wait()

        def one(l, _):
            for i in range(3):
                gf[l, i, ROWS : ROWS + 8, :] = grecv[l, i].astype(F32)[0:8] * not_last
                c = tap(l, i)
                for r in range(0, ROWS, 16):
                    total = c[0] * gf[l, i, r : r + 16, :]
                    for j in range(1, SHORT):
                        total = total + c[j] * gf[l, i, r + j : r + j + 16, :]
                    outv[l, i, r : r + 16, :] = total.astype(BF)
            return 0

        lax.fori_loop(2 * q, 2 * q + 2, one, 0)
        res = []
        for l in (2 * q, 2 * q + 1):
            c = pltpu.make_async_copy(outv.at[l], out.at[:, :, l * 128 : (l + 1) * 128], st_sem.at[l])
            c.start()
            res.append(c)
        return res

    stores = []
    chunk(0)
    chunk(1)
    a0 = gs_zero(0)
    chunk(2)
    gl1 = gl_one()
    a1 = gs_one(0, a0)
    chunk(3)
    b0 = gs_zero(1)
    gl2 = gl_two(gl1)
    stores += conv(0)
    b1 = gs_one(1, b0)
    a2 = gs_two(0, a1)
    stores += conv(1)
    gl3 = gl_three(gl2)
    b2 = gs_two(1, b1)
    stores += conv(2)
    a3 = gs_three(0, a2)
    stores += conv(3)
    b3 = gs_three(1, b2)
    gs_four(0, a3)
    gl_four(gl3)
    gs_four(1, b3)
    for c in stores:
        c.wait()


def solution(mesh):
    n_seq, n_ch = mesh.shape["seq"], mesh.shape["ch"]
    n_z = math.isqrt(n_seq // 2)
    n_y = n_seq // (2 * n_z)
    forward, inverse = transforms()

    def body(features, short_filter, long_filter, grad_out):
        lanes = features.shape[2]
        tiles, chunks, halves = lanes // 128, lanes // 256, lanes // 512
        n_own = 2 * n_ch
        own_rows = TAPS // n_own
        most = max(n_y, n_z, n_own)
        any_spec = pl.BlockSpec(memory_space=pl.ANY)
        vmem = pl.BlockSpec(memory_space=pltpu.VMEM)
        V = pltpu.VMEM
        D = pltpu.SemaphoreType.DMA
        grad_features, grad_short, grad_long = pl.pallas_call(
            functools.partial(kernel, (n_seq, n_ch, n_y, n_z, lanes)),
            out_shape=(
                jax.ShapeDtypeStruct((3, ROWS, lanes), BF),
                jax.ShapeDtypeStruct((3, 8, lanes), F32),
                jax.ShapeDtypeStruct((GROUPS, TAPS), F32),
            ),
            in_specs=[any_spec] * 6,
            out_specs=(any_spec, vmem, vmem),
            scratch_shapes=[
                V((tiles, 3, ROWS, 128), BF),
                V((tiles, ROWS, 128), BF),
                V((N, 2 * N), BF),
                V((ROWS, 2 * N), BF),
                V((3, SHORT, lanes), BF),
                V((GROUPS, TAPS), BF),
                V((tiles, 3, 8, 128), F32),
                V((tiles, 3, ROWS + 8, 128), F32),
                V((tiles, ROWS, 128), BF),
                V((tiles, ROWS, 128), BF),
                V((chunks, ROWS, 256), BF),
                V((chunks, ROWS, 256), BF),
                V((chunks, TAPS, 256), BF),
                V((chunks, TAPS, 256), BF),
                V((3, 16, lanes), BF),
                V((16, lanes), BF),
                V((16, lanes), BF),
                V((tiles, 1, 24, 128), F32),
                V((N, 256), F32),
                V((chunks, N, 256), F32),
                V((chunks, N, 256), F32),
                V((N, 256), F32),
                V((2, N, 256), BF),
                V((N, 512), BF),
                V((N, 512), BF),
                V((ROWS, 512), F32),
                V((tiles, 3, ROWS + 8, 128), F32),
                V((tiles, 3, 16, 128), BF),
                V((tiles, 3, 16, 128), BF),
                V((tiles, 3, ROWS, 128), BF),
                V((TAPS, 256), F32),
                V((n_own - 1, own_rows, 256), F32),
                V((2, own_rows, 128), BF),
                V((2, most - 1, own_rows, 128), BF),
                V((2, own_rows, 128), BF),
                V((2, most - 1, own_rows, 128), BF),
                V((TAPS, 256), F32),
                V((tiles, 24, 128), F32),
                V((halves, 2, 24, 128), F32),
                V((halves, 48, 128), BF),
                V((halves, most - 1, 48, 128), BF),
                V((halves, 48, 128), BF),
                V((halves, most - 1, 48, 128), BF),
                V((tiles, 24, 128), F32),
                D((2 * tiles + 4,)),
                D((tiles,)),
                D((3 + 3 * chunks,)),
                D((3 + 3 * chunks,)),
                D((4, 2, most)),
                D((4, 2, most)),
                D((halves, 4, most)),
                D((halves, 4, most)),
            ],
            compiler_params=pltpu.CompilerParams(
                collective_id=0, has_side_effects=True, vmem_limit_bytes=56 * 2**20
            ),
            name="hyena_backward",
        )(features, short_filter, long_filter, grad_out, jnp.asarray(forward), jnp.asarray(inverse))
        tokens = ROWS * n_seq
        grad_short = grad_short[:, :SHORT, :] / math.sqrt(tokens)
        grad_long = grad_long / math.sqrt(tokens * (lanes * n_ch // GROUPS))
        return grad_features, grad_short, grad_long

    return jax.shard_map(
        body,
        mesh=mesh,
        in_specs=(P(None, "seq", "ch"), P(None, None, "ch"), P(), P("seq", "ch")),
        out_specs=(P(None, "seq", "ch"), P(None, None, "ch"), P()),
        check_vma=False,
    )
```

time: 580 us -> 55.4 us (0.10)
  waiting for transfers between devices: 419 us -> 0 us
  matrix products: 64.6 us -> 0 us
  local copies, waits for them, and re-layouts: 56.2 us -> 2.67 us
  Pallas kernels: 0 us -> 48.8 us
  between operations: 15.9 us -> 0.64 us
  starting transfers between devices: 13.9 us -> 0 us
  other arithmetic: 10 us -> 3.11 us
    psum x2 -> x0, waiting for transfers between devices: 419 us -> none  [the longest x1 262 us: body(): long_total = lax.psum(long_terms, ('seq', 'ch'))]
    conv_general_dilated x6 -> x0, matrix products: 64.6 us -> none  [slide_conv(): lax.conv_general_dilated(signal[None], kernel[:, None, :], (1,), 'VALID',...]
    pallas_call x0 -> x1, Pallas kernels: none -> 48.8 us  [body(): pl.pallas_call(functools.partial(kernel, (n_seq, n_ch, n_y, n_z, lanes)),...]
    reshape x10 -> x0, local copies, waits for them, and re-layouts: 24.4 us -> none  [the longest x9 24.1 us: slide_conv(): lax.conv_general_dilated(signal[None], kernel[:, None, :], (1,), 'VALID',...]
    ppermute x4 -> x0, starting transfers between devices: 13.8 us -> none  [from_behind(): lax.ppermute(value, axis, [(source, source + steps) for source in range(i...]
    convert_element_type x11 -> x0, local copies, waits for them, and re-layouts: 10.4 us -> none  [the longest x6 5.61 us: body(): featured = jax.vmap(slide_conv)(pre_ext, flipped).astype(jnp.bfloat16)]
    rev x4 -> x0, local copies, waits for them, and re-layouts: 6.41 us -> none  [the longest x1 2.92 us: body(): flipped = short_filter[:, ::-1, :]]
    conv_general_dilated x6 -> x0, local copies, waits for them, and re-layouts: 5.9 us -> none  [slide_conv(): lax.conv_general_dilated(signal[None], kernel[:, None, :], (1,), 'VALID',...]
  transfers between devices with their start and end apart: 6 -> 0, of which waited for: 2 -> 0; matrix products, arithmetic and copies ran while one was open for 18% -> 0% of each run, Pallas kernels for 0% -> 0%
where the time goes in v1:
time: 55.4 us; the launch traced here: 55.2 us
  Pallas kernels  48.8 us (88%)
  other arithmetic  3.11 us (6%)
  local copies, waits for them, and re-layouts  2.67 us (5%)
  between operations  0.64 us (1%)
    pallas_call x1, Pallas kernels, body(): pl.pallas_call(functools.partial(kernel, (n_seq, n_ch, n_y, n_z, lanes)),...  48.8 us
    unnamed x1, local copies, waits for them, and re-layouts  2.67 us
    div x1, other arithmetic, body(): grad_long = grad_long / math.sqrt(tokens * (lanes * n_ch // GROUPS))  1.57 us
    div x1, other arithmetic, body(): grad_short = grad_short[:, :SHORT, :] / math.sqrt(tokens)  1.54 us

profile of v1, /device:TPU:1, one launch (start us, length us, event | category | flops | bytes accessed | tf_op | source)
XLA Modules:
  0.0 55.2 jit_solution(17678306386673482478)
XLA Ops:
  0.6 48.8 %hyena_backward.1 = (bf16[3,256,1024]{2,1,0:T(8,128)(2,1)}, f32[3,8,1024]{2,1,0:T(8,128)}, f32[256,128]{1,0:T(8,128)}) custom-call(bf16[3,256,1024]{2,1,0:T(8,128)(2,1)} %feat.1, bf16[3,7,1024]{2,1,0:T(8,128)(2,1)} %short.1, bf16[256,128]{1,0:T(8,128)(2,1)} %long.1, bf16[256,1024]{1,0:T(8,128)(2,1)} %gout.1, bf16[384,768]{1,0:T(8,128)(2,1)} %constant.10.clone.fwd, ...), custom_call_target="tpu_custom_call" | custom-call | tf_op jit(solution)/shard_map/hyena_backward/pallas_call | solution.py:551
  49.4 1.5 %slice_multiply_fusion = f32[3,7,1024]{2,1,0:T(8,128)} fusion(f32[3,8,1024]{2,1,0:T(8,128)} %get-tuple-element.7), kind=kLoop, calls=%fused_computation | loop fusion | flops 21504 | bytes 172032 | tf_op jit(solution)/shard_map/div | solution.py:620
  50.9 1.6 %broadcast_multiply_fusion = f32[256,128]{1,0:T(8,128)} fusion(f32[256,128]{1,0:T(8,128)} %get-tuple-element.8), kind=kLoop, calls=%fused_computation.1 | loop fusion | flops 32768 | bytes 262144 | tf_op jit(solution)/shard_map/div | solution.py:621
  52.5 2.7 %copy.10 = bf16[3,256,1024]{2,1,0:T(8,128)(2,1)} copy(bf16[3,256,1024]{2,1,0:T(8,128)(2,1)} %get-tuple-element.12) | data formatting | bytes 3145728

commit v2 on v1

v2 whole, which is shorter than its diff:
```python
import functools
import math

import jax
import jax.numpy as jnp
import ml_dtypes
import numpy as np
from jax import lax
from jax.experimental import pallas as pl
from jax.experimental.pallas import tpu as pltpu
from jax.sharding import PartitionSpec as P

MESH = pl.DeviceIdType.MESH
BF = jnp.bfloat16
F32 = jnp.float32
ROWS = 256
TAPS = 128
SHORT = 7
GROUPS = 256
N = ROWS + TAPS
HALF = N // 2


def split(matrix):
    high = matrix.astype(ml_dtypes.bfloat16)
    low = (matrix - high.astype(np.float64)).astype(ml_dtypes.bfloat16)
    return high, low


def transforms():
    angle = 2 * np.pi * (np.arange(HALF) + 0.5) / N

    def rows(tokens):
        phase = np.outer(angle, tokens)
        return np.concatenate([np.cos(phase), -np.sin(phase)], axis=0)

    local = rows(np.arange(ROWS))
    behind = rows(np.arange(-TAPS, 0))
    forward = np.concatenate([*split(local), *split(behind)], axis=1)
    inverse = np.concatenate(split(local.T / HALF), axis=1)
    return forward, inverse


def kernel(
    dims,
    feat,
    short,
    long,
    gout,
    fwd,
    inv,
    out,
    gs_out,
    gl_out,
    fb,
    gob,
    fwdv,
    invv,
    shortv,
    longv,
    coef,
    xf,
    kb,
    vb,
    prod,
    gfil,
    xhalo,
    yhalo,
    raw,
    qn,
    hs,
    xs,
    ys,
    rs,
    shi,
    slo,
    filt,
    gf,
    gsend,
    grecv,
    glp,
    glrecv,
    glb,
    glex,
    glmid,
    glex2,
    glfin,
    gsp,
    gscore,
    gsb,
    gsex,
    gsmid,
    gsex2,
    gsfin,
    ld_sem,
    halo_s,
    raw_r,
    x_r,
    y_r,
    g_r,
    gl_s,
    gl_r,
    gs_s,
    gs_r,
):
    n_seq, n_ch, n_y, n_z, lanes = dims
    tokens = ROWS * n_seq
    gs_scale = 1.0 / math.sqrt(tokens)
    gl_scale = 1.0 / math.sqrt(tokens * (lanes * n_ch // GROUPS))
    tiles = lanes // 128
    chunks = lanes // 256
    halves = tiles // 4
    s = lax.axis_index("seq")
    ch = lax.axis_index("ch")
    core = lax.rem(s, 2)
    z = lax.rem(s // 2, n_z)
    y = s // (2 * n_z)

    def at(yy, zz, cc):
        return (yy * n_z + zz) * 2 + cc

    ahead = {"seq": lax.rem(s + 1, n_seq)}
    behind = {"seq": lax.rem(s + n_seq - 1, n_seq)}
    sibling = {"seq": at(y, z, 1 - core)}
    ys_peers = [{"seq": at(lax.rem(y + d, n_y), z, core)} for d in range(1, n_y)]
    zs_peers = [{"seq": at(y, lax.rem(z + d, n_z), core)} for d in range(1, n_z)]
    n_own = 2 * n_ch
    own = ch * 2 + core
    xc_peers = []
    for d in range(1, n_own):
        o = lax.rem(own + d, n_own)
        xc_peers.append(({"seq": at(y, z, lax.rem(o, 2)), "ch": o // 2}, o))

    barrier = pltpu.get_barrier_semaphore()
    greet = [ahead, behind] + ys_peers + zs_peers + [p for p, _ in xc_peers]
    for p in greet:
        pl.semaphore_signal(barrier, inc=1, device_id=p, device_id_type=MESH)

    def load(src, dst, i):
        c = pltpu.make_async_copy(src, dst, ld_sem.at[i])
        c.start()
        return c

    def all_of(ref, sem):
        pltpu.make_async_copy(ref, ref, sem).wait()

    c_short = load(short, shortv, 0)
    for l in range(tiles):
        load(feat.at[:, :, l * 128 : (l + 1) * 128], fb.at[l], 1)
    for l in range(tiles):
        load(gout.at[:, l * 128 : (l + 1) * 128], gob.at[l], 2)
    c_long = load(long, longv, 3)
    c_fwd = load(fwd, fwdv, 4)
    c_inv = load(inv, invv, 5)

    def remote(src, dst, ssem, rsem, peer):
        pltpu.make_async_remote_copy(
            src_ref=src, dst_ref=dst, send_sem=ssem, recv_sem=rsem, device_id=peer, device_id_type=MESH
        ).start()

    c_short.wait()
    for i in range(3):
        taps = shortv[i].astype(F32)
        for l in range(tiles):
            coef[l, i, 0:SHORT, :] = taps[:, l * 128 : (l + 1) * 128]
    all_of(fb, ld_sem.at[1])

    def tap(l, i):
        return [coef[l, i, j : j + 1, :] for j in range(SHORT)]

    def fir(ref, l, i, c, first):
        total = c[0] * ref[l, i, first : first + 16, :]
        for j in range(1, SHORT):
            total = total + c[j] * ref[l, i, first - j : first - j + 16, :]
        return total.astype(BF)

    def widen(l, i, lo, hi):
        for r in range(lo, hi, 16):
            xf[l, i, 8 + r : 24 + r, :] = fb[l, i, r : r + 16, :].astype(F32)

    def tile(l):
        return pl.ds(pl.multiple_of(l * 128, 128), 128)

    def lane(l):
        return pl.ds(pl.multiple_of(lax.rem(l, 2) * 128, 128), 128)

    def product_rows(l, lo, hi):
        ck, cv = tap(l, 1), tap(l, 2)
        for r in range(lo, hi, 16):
            k = fir(xf, l, 1, ck, 8 + r)
            v = fir(xf, l, 2, cv, 8 + r)
            kb[l, r : r + 16, :] = k
            vb[l, r : r + 16, :] = v
            prod[l // 2, r : r + 16, lane(l)] = (k.astype(F32) * v.astype(F32)).astype(BF)

    def grad_rows(l, lo, hi):
        cq = tap(l, 0)
        for r in range(lo, hi, 16):
            q = fir(xf, l, 0, cq, 8 + r)
            gfil[l // 2, r : r + 16, lane(l)] = (
                q.astype(F32) * gob[l, r : r + 16, :].astype(F32)
            ).astype(BF)

    def tail(l, _):
        widen(l, 1, 112, ROWS)
        widen(l, 2, 112, ROWS)
        product_rows(l, 128, ROWS)
        return 0

    def tails():
        lax.fori_loop(0, tiles, tail, 0)

    raw_s, x_s, y_s, g_s = (halo_s.at[k] for k in range(4))

    def send_first():
        pl.semaphore_wait(barrier, len(greet))
        remote(feat.at[:, ROWS - 16 :, :], raw.at[0:3], raw_s, raw_r.at[0], ahead)
        remote(feat.at[0, 0:16, :], raw.at[3], raw_s, raw_r.at[0], behind)
        remote(gout.at[0:16, :], raw.at[4], raw_s, raw_r.at[0], behind)
        for q in range(chunks):
            remote(prod.at[q, ROWS - TAPS :, :], xhalo.at[q], x_s, x_r.at[q], ahead)

    def head(l, _):
        widen(l, 0, 0, 128)
        grad_rows(l, 16, 128)
        return 0

    def heads(q):
        lax.fori_loop(2 * q, 2 * q + 2, head, 0)

    def send_head(q):
        remote(gfil.at[q, 16:TAPS, :], yhalo.at[q, 16:TAPS, :], y_s, y_r.at[q], behind)

    def rest(l, _):
        widen(l, 0, 128, ROWS)
        grad_rows(l, 128, ROWS)
        widen(l, 1, 0, 112)
        widen(l, 2, 0, 112)
        product_rows(l, 16, 128)
        return 0

    def rests():
        lax.fori_loop(0, tiles, rest, 0)

    nt = (((1,), (1,)), ((), ()))

    def spectrum():
        hs[...] = lax.dot_general(fwdv[:, 0:TAPS], longv[...], nt, preferred_element_type=F32) + lax.dot_general(
        fwdv[:, ROWS : ROWS + TAPS], longv[...], nt, preferred_element_type=F32
    )

    not_first = jnp.where(s > 0, 1.0, 0.0).astype(F32)
    not_last = jnp.where(s < n_seq - 1, 1.0, 0.0).astype(F32)
    def edges(l):
        cols = slice(l * 128, (l + 1) * 128)
        for i in range(3):
            xf[l, i, 0:8, :] = raw[i, :, cols].astype(F32)[8:16] * not_first
        qn[l, 0, 0:8, :] = xf[l, 0, ROWS : ROWS + 8, :]
        qn[l, 0, 8:24, :] = raw[3, :, cols].astype(F32)
        product_rows(l, 0, 16)
        grad_rows(l, 0, 16)
        qq = fir(qn, l, 0, tap(l, 0), 8)
        yhalo[l // 2, 0:16, (l % 2) * 128 : (l % 2) * 128 + 128] = (
            qq.astype(F32) * raw[4, :, cols].astype(F32)
        ).astype(BF)

    def dot(a, b):
        return jnp.dot(a, b, preferred_element_type=F32)

    def local(q):
        p = prod[q]
        xs[q] = dot(fwdv[:, 0:ROWS], p) + dot(fwdv[:, ROWS : 2 * ROWS], p)
        g = gfil[q]
        ys[q] = dot(fwdv[:, 0:ROWS], g) + dot(fwdv[:, ROWS : 2 * ROWS], g)


    def far(h):
        return dot(fwdv[:, 2 * ROWS : 2 * ROWS + TAPS], h) + dot(fwdv[:, 2 * ROWS + TAPS :], h)

    def wait_x(q):
        all_of(xhalo.at[q], x_r.at[q])

    def wait_y(q):
        all_of(yhalo.at[q, 16:TAPS, :], y_r.at[q])

    def add_x(q):
        wait_x(q)
        xs[q] = xs[q] + not_first * far(xhalo[q])

    def add_y(q):
        wait_y(q)
        ys[q] = ys[q] - not_last * far(yhalo[q])

    def corr(q, first):
        def block(b, _):
            re = pl.ds(pl.multiple_of(b * 16, 16), 16)
            im = pl.ds(pl.multiple_of(b * 16 + HALF, 16), 16)
            xr, xi, yr, yi = xs[q, re, :], xs[q, im, :], ys[q, re, :], ys[q, im, :]
            rr = xr * yr + xi * yi
            ri = xr * yi - xi * yr
            if not first:
                rr = rr + rs[re, :]
                ri = ri + rs[im, :]
            rs[re, :] = rr
            rs[im, :] = ri
            return 0

        lax.fori_loop(0, HALF // 16, block, 0)

    def hilo(value):
        high = value.astype(BF)
        return high, (value - high.astype(F32)).astype(BF)

    def lags():
        rh, rl = hilo(rs[...])
        glp[...] = (
            dot(invv[0:TAPS, 0:N], rh) + dot(invv[0:TAPS, N:], rh) + dot(invv[0:TAPS, 0:N], rl)
        )

    own_rows = TAPS // n_own
    mine = pl.ds(pl.multiple_of(own * own_rows, own_rows), own_rows)

    def gl_zero():
        for d, (p, o) in enumerate(xc_peers):
            piece = pl.ds(pl.multiple_of(o * own_rows, own_rows), own_rows)
            remote(glp.at[piece, :], glrecv.at[d], gl_s.at[0], gl_r.at[0], p)

    def spread(src, dst, ssem, rsem, peers):
        for d, p in enumerate(peers):
            remote(src, dst.at[d], ssem, rsem, p)

    def gathered(mid, ref, sem, peers):
        all_of(ref.at[0 : len(peers)], sem)
        total = mid.astype(F32)
        for d in range(len(peers)):
            total = total + ref[d].astype(F32)
        return total

    rings = ((ys_peers, zs_peers), (zs_peers, ys_peers))

    def gl_one():
        total = gathered(glp[mine, :], glrecv, gl_r.at[0], xc_peers)
        for k in range(2):
            glb[k] = total[:, k * 128 : (k + 1) * 128].astype(BF)
            spread(glb.at[k], glex.at[k], gl_s.at[1 + k], gl_r.at[1 + k], rings[k][0])

    def gl_two():
        for k in range(2):
            glmid[k] = gathered(glb[k], glex.at[k], gl_r.at[1 + k], rings[k][0]).astype(BF)
            spread(glmid.at[k], glex2.at[k], gl_s.at[3 + k], gl_r.at[3 + k], rings[k][1])

    def gl_three():
        for k in range(2):
            total = gathered(glmid[k], glex2.at[k], gl_r.at[3 + k], rings[k][1])
            glfin[mine, k * 128 : (k + 1) * 128] = total * gl_scale
        for d, (p, _) in enumerate(xc_peers):
            remote(glfin.at[mine, :], glfin.at[mine, :], gl_s.at[5], gl_r.at[5], p)

    def gl_four():
        all_of(glfin.at[0 : TAPS - own_rows], gl_r.at[5])
        gl_out[...] = glfin[...].T

    def gs_zero(h):
        theirs = pl.ds(4 * h + 2 * (1 - core), 2)
        remote(gsp.at[theirs], gscore.at[h], gs_s.at[h, 0], gs_r.at[h, 0], sibling)

    def gs_one(h):
        all_of(gscore.at[h], gs_r.at[h, 0])
        total = gsp[pl.ds(4 * h + 2 * core, 2)] + gscore[h]
        gsb[h] = total.reshape(48, 128).astype(BF)
        spread(gsb.at[h], gsex.at[h], gs_s.at[h, 1], gs_r.at[h, 1], rings[h % 2][0])

    def gs_two(h):
        gsmid[h] = gathered(gsb[h], gsex.at[h], gs_r.at[h, 1], rings[h % 2][0]).astype(BF)
        spread(gsmid.at[h], gsex2.at[h], gs_s.at[h, 2], gs_r.at[h, 2], rings[h % 2][1])

    def gs_three(h):
        total = gathered(gsmid[h], gsex2.at[h], gs_r.at[h, 2], rings[h % 2][1]) * gs_scale
        here = pl.ds(4 * h + 2 * core, 2)
        gsfin[here] = total.reshape(2, 24, 128)
        remote(gsfin.at[here], gsfin.at[here], gs_s.at[h, 3], gs_r.at[h, 3], sibling)

    def gs_four(h):
        all_of(gscore.at[h], gs_r.at[h, 3])
        for l in range(4 * h, 4 * h + 4):
            for i in range(3):
                gs_out[i, :, l * 128 : (l + 1) * 128] = gsfin[l, 8 * i : 8 * i + SHORT, :]

    def spectra(q):
        def block(b, _):
            re = pl.ds(pl.multiple_of(b * 16, 16), 16)
            im = pl.ds(pl.multiple_of(b * 16 + HALF, 16), 16)
            hr, hi = hs[re, :], hs[im, :]
            xr, xi = xs[q, re, :], xs[q, im, :]
            yr, yi = ys[q, re, :], ys[q, im, :]
            parts = (
                (re, 0, xr * hr - xi * hi),
                (im, 0, xr * hi + xi * hr),
                (re, 256, yr * hr + yi * hi),
                (im, 256, yi * hr - yr * hi),
            )
            for rows, c, value in parts:
                high, low = hilo(value)
                shi[rows, c : c + 256] = high
                slo[rows, c : c + 256] = low
            return 0

        lax.fori_loop(0, HALF // 16, block, 0)

    def inverse():
        for c in (0, 256):
            sh = shi[:, c : c + 256]
            filt[:, c : c + 256] = (
                dot(invv[:, 0:N], sh) + dot(invv[:, N:], sh) + dot(invv[:, 0:N], slo[:, c : c + 256])
            )

    def featured_grad(l, h):
        for r in range(0, ROWS, 16):
            rows = slice(r, r + 16)
            fa = filt[rows, h * 128 : h * 128 + 128]
            fg = filt[rows, 256 + h * 128 : 256 + h * 128 + 128]
            g0 = (gob[l, rows, :].astype(F32) * fa).astype(BF)
            g1 = (fg * vb[l, rows, :].astype(F32)).astype(BF)
            g2 = (fg * kb[l, rows, :].astype(F32)).astype(BF)
            for i, g in enumerate((g0, g1, g2)):
                gf[l, i, rows, :] = g.astype(F32)
                if r == 0:
                    gsend[l, i] = g

    def short_grad(l):
        for i in range(3):
            acc = [jnp.zeros((8, 128), F32) for _ in range(SHORT)]
            for r in range(0, ROWS, 8):
                g = gf[l, i, r : r + 8, :]
                for j in range(SHORT):
                    acc[j] = acc[j] + g * xf[l, i, 8 + r - j : 16 + r - j, :]
            rows = [jnp.sum(a, axis=0, keepdims=True) for a in acc]
            rows.append(jnp.zeros((1, 128), F32))
            gsp[l, 8 * i : 8 * i + 8, :] = jnp.concatenate(rows, axis=0)

    def fgrads(q):
        for h in range(2):
            featured_grad(2 * q + h, h)

    def send_grad(q):
        two = pl.ds(2 * q, 2)
        remote(gsend.at[two], grecv.at[two], g_s, g_r.at[q], behind)

    def sgrads(q):
        def sg(l, _):
            short_grad(l)
            return 0

        lax.fori_loop(2 * q, 2 * q + 2, sg, 0)

    def wait_grad(q):
        all_of(grecv.at[pl.ds(2 * q, 2)], g_r.at[q])

    def conv(q):
        wait_grad(q)

        def one(l, _):
            for i in range(3):
                gf[l, i, ROWS : ROWS + 8, :] = grecv[l, i].astype(F32)[0:8] * not_last
                c = tap(l, i)
                for r in range(0, ROWS, 16):
                    total = c[0] * gf[l, i, r : r + 16, :]
                    for j in range(1, SHORT):
                        total = total + c[j] * gf[l, i, r + j : r + j + 16, :]
                    out[i, r : r + 16, tile(l)] = total.astype(BF)
            return 0

        lax.fori_loop(2 * q, 2 * q + 2, one, 0)

    tails()
    send_first()
    all_of(gob, ld_sem.at[2])
    order = list(range(chunks // 2, chunks)) + list(range(chunks // 2))
    for q in order:
        heads(q)
        send_head(q)
    rests()
    c_long.wait()
    c_fwd.wait()
    spectrum()
    all_of(raw, raw_r.at[0])
    for l in range(tiles):
        edges(l)
    for q in range(chunks):
        local(q)
    for q in range(chunks // 2):
        add_x(q)
        corr(q, q == 0)
    for q in range(chunks // 2, chunks):
        add_y(q)
        corr(q, False)
    c_inv.wait()
    lags()
    gl_zero()

    def chunk(q):
        if q < chunks // 2:
            add_y(q)
        else:
            add_x(q)
        spectra(q)
        inverse()
        fgrads(q)
        send_grad(q)
        sgrads(q)

    chunk(0)
    chunk(1)
    gs_zero(0)
    chunk(2)
    gl_one()
    gs_one(0)
    chunk(3)
    gs_zero(1)
    gl_two()
    conv(0)
    gs_one(1)
    gs_two(0)
    conv(1)
    gl_three()
    gs_two(1)
    conv(2)
    gs_three(0)
    conv(3)
    gs_three(1)
    gs_four(0)
    gl_four()
    gs_four(1)

    all_of(raw, raw_s)
    all_of(xhalo, x_s)
    all_of(yhalo.at[:, 16:TAPS, :], y_s)
    all_of(grecv, g_s)
    all_of(glrecv, gl_s.at[0])
    for k in range(2):
        all_of(glex.at[k, 0 : len(rings[k][0])], gl_s.at[1 + k])
        all_of(glex2.at[k, 0 : len(rings[k][1])], gl_s.at[3 + k])
    all_of(glrecv, gl_s.at[5])
    for h in range(halves):
        all_of(gscore.at[h], gs_s.at[h, 0])
        all_of(gsex.at[h, 0 : len(rings[h % 2][0])], gs_s.at[h, 1])
        all_of(gsex2.at[h, 0 : len(rings[h % 2][1])], gs_s.at[h, 2])
        all_of(gscore.at[h], gs_s.at[h, 3])


def solution(mesh):
    n_seq, n_ch = mesh.shape["seq"], mesh.shape["ch"]
    n_z = math.isqrt(n_seq // 2)
    n_y = n_seq // (2 * n_z)
    forward, inverse = transforms()

    def body(features, short_filter, long_filter, grad_out):
        lanes = features.shape[2]
        tiles, chunks, halves = lanes // 128, lanes // 256, lanes // 512
        n_own = 2 * n_ch
        own_rows = TAPS // n_own
        most = max(n_y, n_z)
        any_spec = pl.BlockSpec(memory_space=pltpu.HBM)
        vmem = pl.BlockSpec(memory_space=pltpu.VMEM)
        V = pltpu.VMEM
        D = pltpu.SemaphoreType.DMA
        grad_features, grad_short, grad_long = pl.pallas_call(
            functools.partial(kernel, (n_seq, n_ch, n_y, n_z, lanes)),
            out_shape=(
                V((3, ROWS, lanes), BF),
                V((3, SHORT, lanes), F32),
                V((GROUPS, TAPS), F32),
            ),
            in_specs=[any_spec] * 6,
            out_specs=(vmem, vmem, vmem),
            scratch_shapes=[
                V((tiles, 3, ROWS, 128), BF),
                V((tiles, ROWS, 128), BF),
                V((N, 2 * N), BF),
                V((ROWS, 2 * N), BF),
                V((3, SHORT, lanes), BF),
                V((GROUPS, TAPS), BF),
                V((tiles, 3, 8, 128), F32),
                V((tiles, 3, ROWS + 8, 128), F32),
                V((tiles, ROWS, 128), BF),
                V((tiles, ROWS, 128), BF),
                V((chunks, ROWS, 256), BF),
                V((chunks, ROWS, 256), BF),
                V((chunks, TAPS, 256), BF),
                V((chunks, TAPS, 256), BF),
                V((5, 16, lanes), BF),
                V((tiles, 1, 24, 128), F32),
                V((N, 256), F32),
                V((chunks, N, 256), F32),
                V((chunks, N, 256), F32),
                V((N, 256), F32),
                V((N, 512), BF),
                V((N, 512), BF),
                V((ROWS, 512), F32),
                V((tiles, 3, ROWS + 8, 128), F32),
                V((tiles, 3, 16, 128), BF),
                V((tiles, 3, 16, 128), BF),
                V((TAPS, 256), F32),
                V((n_own - 1, own_rows, 256), F32),
                V((2, own_rows, 128), BF),
                V((2, most - 1, own_rows, 128), BF),
                V((2, own_rows, 128), BF),
                V((2, most - 1, own_rows, 128), BF),
                V((TAPS, 256), F32),
                V((tiles, 24, 128), F32),
                V((halves, 2, 24, 128), F32),
                V((halves, 48, 128), BF),
                V((halves, most - 1, 48, 128), BF),
                V((halves, 48, 128), BF),
                V((halves, most - 1, 48, 128), BF),
                V((tiles, 24, 128), F32),
                D((6,)),
                D((4,)),
                D((1,)),
                D((chunks,)),
                D((chunks,)),
                D((chunks,)),
                D((6,)),
                D((6,)),
                D((halves, 4)),
                D((halves, 4)),
            ],
            compiler_params=pltpu.CompilerParams(
                collective_id=0, has_side_effects=True, vmem_limit_bytes=40 * 2**20
            ),
            name="hyena_backward",
        )(
            *(
                pltpu.with_memory_space_constraint(a, pltpu.HBM)
                for a in (features, short_filter, long_filter, grad_out, jnp.asarray(forward), jnp.asarray(inverse))
            )
        )
        return grad_features, grad_short, grad_long

    return jax.shard_map(
        body,
        mesh=mesh,
        in_specs=(P(None, "seq", "ch"), P(None, None, "ch"), P(), P("seq", "ch")),
        out_specs=(P(None, "seq", "ch"), P(None, None, "ch"), P()),
        check_vma=False,
    )
```

time: 55.4 us -> 48.4 us (0.87)
  Pallas kernels: 48.8 us -> 45.2 us
  other arithmetic: 3.11 us -> 0 us
    pallas_call x1, Pallas kernels: 48.8 us -> 45.2 us  [body(): pl.pallas_call(functools.partial(kernel, (n_seq, n_ch, n_y, n_z, lanes)),...]
    div x2 -> x0, other arithmetic: 3.11 us -> none  [the longest x1 1.57 us: body(): grad_long = grad_long / math.sqrt(tokens * (lanes * n_ch // GROUPS))]
    unnamed x1 -> x3, local copies, waits for them, and re-layouts: 2.67 us -> 2.44 us
where the time goes in v2:
time: 48.4 us; the launch traced here: 48.3 us
  Pallas kernels  45.2 us (93%)
  local copies, waits for them, and re-layouts  2.44 us (5%)
  between operations  0.64 us (1%)
    pallas_call x1, Pallas kernels, body(): pl.pallas_call(functools.partial(kernel, (n_seq, n_ch, n_y, n_z, lanes)),...  45.2 us
    unnamed x3, local copies, waits for them, and re-layouts  2.44 us

profile of v2, /device:TPU:1, one launch (start us, length us, event | category | flops | bytes accessed | tf_op | source)
XLA Modules:
  0.0 48.3 jit_solution(16016272141520212803)
XLA Ops:
  0.6 45.2 %hyena_backward.1 = (bf16[3,256,1024]{2,1,0:T(8,128)(2,1)S(1)}, f32[3,7,1024]{2,1,0:T(8,128)S(1)}, f32[256,128]{1,0:T(8,128)S(1)}) custom-call(bf16[3,256,1024]{2,1,0:T(8,128)(2,1)} %feat.1, bf16[3,7,1024]{2,1,0:T(8,128)(2,1)} %short.1, bf16[256,128]{1,0:T(8,128)(2,1)} %long.1, bf16[256,1024]{1,0:T(8,128)(2,1)} %gout.1, bf16[384,768]{1,0:T(8,128)(2,1)} %constant.4.clone.fwd, ...), custom_call_target="tpu_custom_call" | custom-call | tf_op jit(solution)/shard_map/hyena_backward/pallas_call | solution.py:567
  45.9 1.1 %copy.12 = bf16[3,256,1024]{2,1,0:T(8,128)(2,1)} copy(bf16[3,256,1024]{2,1,0:T(8,128)(2,1)S(1)} %get-tuple-element.3) | data formatting | bytes 3145728
  47.0 0.6 %copy.13 = f32[3,7,1024]{2,1,0:T(8,128)} copy(f32[3,7,1024]{2,1,0:T(8,128)S(1)} %get-tuple-element.4) | data formatting | bytes 172032
  47.6 0.7 %copy.14 = f32[256,128]{1,0:T(8,128)} copy(f32[256,128]{1,0:T(8,128)S(1)} %get-tuple-element.5) | data formatting | bytes 262144

commit v3 on v2

--- a/solution.py
+++ b/solution.py
@@ -16,6 +16,7 @@
 ROWS = 256
 TAPS = 128
 SHORT = 7
+EDGE = SHORT - 1
 GROUPS = 256
 N = ROWS + TAPS
 HALF = N // 2
@@ -67,34 +68,30 @@
     xhalo,
     yhalo,
     raw,
+    packf,
+    packb,
     qn,
     hs,
     xs,
     ys,
     rs,
-    shi,
-    slo,
+    spec,
     filt,
     gf,
-    gsend,
-    grecv,
+    gpack,
+    gedge,
     glp,
     glrecv,
-    glb,
     glex,
-    glmid,
     glex2,
     glfin,
     gsp,
     gscore,
-    gsb,
     gsex,
-    gsmid,
     gsex2,
     gsfin,
     ld_sem,
     halo_s,
-    raw_r,
     x_r,
     y_r,
     g_r,
@@ -122,8 +119,12 @@
     ahead = {"seq": lax.rem(s + 1, n_seq)}
     behind = {"seq": lax.rem(s + n_seq - 1, n_seq)}
     sibling = {"seq": at(y, z, 1 - core)}
-    ys_peers = [{"seq": at(lax.rem(y + d, n_y), z, core)} for d in range(1, n_y)]
-    zs_peers = [{"seq": at(y, lax.rem(z + d, n_z), core)} for d in range(1, n_z)]
+
+    def far_first(n):
+        return sorted(range(1, n), key=lambda d: -min(d, n - d))
+
+    ys_peers = [{"seq": at(lax.rem(y + d, n_y), z, core)} for d in far_first(n_y)]
+    zs_peers = [{"seq": at(y, lax.rem(z + d, n_z), core)} for d in far_first(n_z)]
     n_own = 2 * n_ch
     own = ch * 2 + core
     xc_peers = []
@@ -202,6 +203,7 @@
             ).astype(BF)
 
     def tail(l, _):
+        widen(l, 0, ROWS - 16, ROWS)
         widen(l, 1, 112, ROWS)
         widen(l, 2, 112, ROWS)
         product_rows(l, 128, ROWS)
@@ -210,13 +212,22 @@
     def tails():
         lax.fori_loop(0, tiles, tail, 0)
 
-    raw_s, x_s, y_s, g_s = (halo_s.at[k] for k in range(4))
+    raw_s, pack_s, x_s, y_s, g_s, raw_r, pack_r = (halo_s.at[k] for k in range(7))
+
+    def six(l, i):
+        return slice((3 * l + i) * EDGE, (3 * l + i + 1) * EDGE)
+
+    def packs():
+        for l in range(tiles):
+            for i in range(3):
+                packf[six(l, i), :] = xf[l, i, 8 + ROWS - EDGE : 8 + ROWS, :]
+        packb[0] = packf[...].astype(BF)
 
     def send_first():
         pl.semaphore_wait(barrier, len(greet))
-        remote(feat.at[:, ROWS - 16 :, :], raw.at[0:3], raw_s, raw_r.at[0], ahead)
-        remote(feat.at[0, 0:16, :], raw.at[3], raw_s, raw_r.at[0], behind)
-        remote(gout.at[0:16, :], raw.at[4], raw_s, raw_r.at[0], behind)
+        remote(packb.at[0], packb.at[1], pack_s, pack_r, ahead)
+        remote(feat.at[0, 0:16, :], raw.at[0], raw_s, raw_r, behind)
+        remote(gout.at[0:16, :], raw.at[1], raw_s, raw_r, behind)
         for q in range(chunks):
             remote(prod.at[q, ROWS - TAPS :, :], xhalo.at[q], x_s, x_r.at[q], ahead)
 
@@ -251,17 +262,20 @@
 
     not_first = jnp.where(s > 0, 1.0, 0.0).astype(F32)
     not_last = jnp.where(s < n_seq - 1, 1.0, 0.0).astype(F32)
+    def unpack():
+        packf[...] = packb[1].astype(F32) * not_first
+
     def edges(l):
         cols = slice(l * 128, (l + 1) * 128)
         for i in range(3):
-            xf[l, i, 0:8, :] = raw[i, :, cols].astype(F32)[8:16] * not_first
+            xf[l, i, 8 - EDGE : 8, :] = packf[six(l, i), :]
         qn[l, 0, 0:8, :] = xf[l, 0, ROWS : ROWS + 8, :]
-        qn[l, 0, 8:24, :] = raw[3, :, cols].astype(F32)
+        qn[l, 0, 8:24, :] = raw[0, :, cols].astype(F32)
         product_rows(l, 0, 16)
         grad_rows(l, 0, 16)
         qq = fir(qn, l, 0, tap(l, 0), 8)
         yhalo[l // 2, 0:16, (l % 2) * 128 : (l % 2) * 128 + 128] = (
-            qq.astype(F32) * raw[4, :, cols].astype(F32)
+            qq.astype(F32) * raw[1, :, cols].astype(F32)
         ).astype(BF)
 
     def dot(a, b):
@@ -311,77 +325,96 @@
         high = value.astype(BF)
         return high, (value - high.astype(F32)).astype(BF)
 
+    own_rows = TAPS // n_own
+
+    def piece(o):
+        return pl.ds(pl.multiple_of(o * own_rows, own_rows), own_rows)
+
     def lags():
         rh, rl = hilo(rs[...])
         glp[...] = (
             dot(invv[0:TAPS, 0:N], rh) + dot(invv[0:TAPS, N:], rh) + dot(invv[0:TAPS, 0:N], rl)
-        )
-
-    own_rows = TAPS // n_own
-    mine = pl.ds(pl.multiple_of(own * own_rows, own_rows), own_rows)
-
-    def gl_zero():
-        for d, (p, o) in enumerate(xc_peers):
-            piece = pl.ds(pl.multiple_of(o * own_rows, own_rows), own_rows)
-            remote(glp.at[piece, :], glrecv.at[d], gl_s.at[0], gl_r.at[0], p)
-
-    def spread(src, dst, ssem, rsem, peers):
-        for d, p in enumerate(peers):
-            remote(src, dst.at[d], ssem, rsem, p)
-
-    def gathered(mid, ref, sem, peers):
-        all_of(ref.at[0 : len(peers)], sem)
-        total = mid.astype(F32)
-        for d in range(len(peers)):
+        ).astype(BF)
+
+    rings = ((ys_peers, zs_peers), (zs_peers, ys_peers))
+    places = ((y, z), (z, y))
+
+    def spread(ref, place, value, ssem, rsem, peers):
+        ref[place] = value
+        for p in peers:
+            remote(ref.at[place], ref.at[place], ssem, rsem, p)
+
+    def gathered(ref, sem, count):
+        all_of(ref.at[0 : count - 1], sem)
+        total = ref[0].astype(F32)
+        for d in range(1, count):
             total = total + ref[d].astype(F32)
         return total
 
-    rings = ((ys_peers, zs_peers), (zs_peers, ys_peers))
+    counts = ((n_y, n_z), (n_z, n_y))
+
+    def gl_zero():
+        glrecv[own] = glp[piece(own), :]
+        for p, o in xc_peers:
+            remote(glp.at[piece(o), :], glrecv.at[own], gl_s.at[0], gl_r.at[0], p)
 
     def gl_one():
-        total = gathered(glp[mine, :], glrecv, gl_r.at[0], xc_peers)
+        total = gathered(glrecv, gl_r.at[0], n_own)
         for k in range(2):
-            glb[k] = total[:, k * 128 : (k + 1) * 128].astype(BF)
-            spread(glb.at[k], glex.at[k], gl_s.at[1 + k], gl_r.at[1 + k], rings[k][0])
-
-    def gl_two():
-        for k in range(2):
-            glmid[k] = gathered(glb[k], glex.at[k], gl_r.at[1 + k], rings[k][0]).astype(BF)
-            spread(glmid.at[k], glex2.at[k], gl_s.at[3 + k], gl_r.at[3 + k], rings[k][1])
+            part = total[:, k * 128 : (k + 1) * 128].astype(BF)
+            spread(glex.at[k], places[k][0], part, gl_s.at[1 + k], gl_r.at[1 + k], rings[k][0])
+
+    def gl_two(k):
+        part = gathered(glex.at[k], gl_r.at[1 + k], counts[k][0]).astype(BF)
+        spread(glex2.at[k], places[k][1], part, gl_s.at[3 + k], gl_r.at[3 + k], rings[k][1])
 
     def gl_three():
         for k in range(2):
-            total = gathered(glmid[k], glex2.at[k], gl_r.at[3 + k], rings[k][1])
-            glfin[mine, k * 128 : (k + 1) * 128] = total * gl_scale
-        for d, (p, _) in enumerate(xc_peers):
-            remote(glfin.at[mine, :], glfin.at[mine, :], gl_s.at[5], gl_r.at[5], p)
+            total = gathered(glex2.at[k], gl_r.at[3 + k], counts[k][1]) * gl_scale
+            glfin[piece(own), k * 128 : (k + 1) * 128] = total.astype(BF)
+        for p, _ in xc_peers:
+            remote(glfin.at[piece(own), :], glfin.at[piece(own), :], gl_s.at[5], gl_r.at[5], p)
 
     def gl_four():
         all_of(glfin.at[0 : TAPS - own_rows], gl_r.at[5])
-        gl_out[...] = glfin[...].T
+        gl_out[...] = glfin[...].astype(F32).T
 
     def gs_zero(h):
         theirs = pl.ds(4 * h + 2 * (1 - core), 2)
         remote(gsp.at[theirs], gscore.at[h], gs_s.at[h, 0], gs_r.at[h, 0], sibling)
 
+    def part_rows(h, k):
+        cut = 32 if h % 2 == 0 else 16
+        return slice(0, cut) if k == 0 else slice(cut, 48)
+
     def gs_one(h):
         all_of(gscore.at[h], gs_r.at[h, 0])
         total = gsp[pl.ds(4 * h + 2 * core, 2)] + gscore[h]
-        gsb[h] = total.reshape(48, 128).astype(BF)
-        spread(gsb.at[h], gsex.at[h], gs_s.at[h, 1], gs_r.at[h, 1], rings[h % 2][0])
+        total = total.reshape(48, 128)
+        for k in range(2):
+            rows = part_rows(h, k)
+            ref = gsex.at[h, :, rows, :]
+            spread(ref, places[k][0], total[rows].astype(BF), gs_s.at[h, 1 + k], gs_r.at[h, 1 + k], rings[k][0])
 
     def gs_two(h):
-        gsmid[h] = gathered(gsb[h], gsex.at[h], gs_r.at[h, 1], rings[h % 2][0]).astype(BF)
-        spread(gsmid.at[h], gsex2.at[h], gs_s.at[h, 2], gs_r.at[h, 2], rings[h % 2][1])
+        for k in range(2):
+            rows = part_rows(h, k)
+            part = gathered(gsex.at[h, :, rows, :], gs_r.at[h, 1 + k], counts[k][0]).astype(BF)
+            ref = gsex2.at[h, :, rows, :]
+            spread(ref, places[k][1], part, gs_s.at[h, 3 + k], gs_r.at[h, 3 + k], rings[k][1])
 
     def gs_three(h):
-        total = gathered(gsmid[h], gsex2.at[h], gs_r.at[h, 2], rings[h % 2][1]) * gs_scale
+        parts = []
+        for k in range(2):
+            ref = gsex2.at[h, :, part_rows(h, k), :]
+            parts.append(gathered(ref, gs_r.at[h, 3 + k], counts[k][1]))
+        total = jnp.concatenate(parts, axis=0) * gs_scale
         here = pl.ds(4 * h + 2 * core, 2)
         gsfin[here] = total.reshape(2, 24, 128)
-        remote(gsfin.at[here], gsfin.at[here], gs_s.at[h, 3], gs_r.at[h, 3], sibling)
+        remote(gsfin.at[here], gsfin.at[here], gs_s.at[h, 5], gs_r.at[h, 5], sibling)
 
     def gs_four(h):
-        all_of(gscore.at[h], gs_r.at[h, 3])
+        all_of(gscore.at[h], gs_r.at[h, 5])
         for l in range(4 * h, 4 * h + 4):
             for i in range(3):
                 gs_out[i, :, l * 128 : (l + 1) * 128] = gsfin[l, 8 * i : 8 * i + SHORT, :]
@@ -400,19 +433,13 @@
                 (im, 256, yi * hr - yr * hi),
             )
             for rows, c, value in parts:
-                high, low = hilo(value)
-                shi[rows, c : c + 256] = high
-                slo[rows, c : c + 256] = low
+                spec[rows, c : c + 256] = value.astype(BF)
             return 0
 
         lax.fori_loop(0, HALF // 16, block, 0)
 
     def inverse():
-        for c in (0, 256):
-            sh = shi[:, c : c + 256]
-            filt[:, c : c + 256] = (
-                dot(invv[:, 0:N], sh) + dot(invv[:, N:], sh) + dot(invv[:, 0:N], slo[:, c : c + 256])
-            )
+        filt[...] = dot(invv[:, 0:N], spec[...])
 
     def featured_grad(l, h):
         for r in range(0, ROWS, 16):
@@ -424,8 +451,6 @@
             g2 = (fg * kb[l, rows, :].astype(F32)).astype(BF)
             for i, g in enumerate((g0, g1, g2)):
                 gf[l, i, rows, :] = g.astype(F32)
-                if r == 0:
-                    gsend[l, i] = g
 
     def short_grad(l):
         for i in range(3):
@@ -443,8 +468,11 @@
             featured_grad(2 * q + h, h)
 
     def send_grad(q):
-        two = pl.ds(2 * q, 2)
-        remote(gsend.at[two], grecv.at[two], g_s, g_r.at[q], behind)
+        for h in range(2):
+            for i in range(3):
+                gpack[six(h, i), :] = gf[2 * q + h, i, 0:EDGE, :]
+        gedge[0, q] = gpack[...].astype(BF)
+        remote(gedge.at[0, q], gedge.at[1, q], g_s, g_r.at[q], behind)
 
     def sgrads(q):
         def sg(l, _):
@@ -454,14 +482,17 @@
         lax.fori_loop(2 * q, 2 * q + 2, sg, 0)
 
     def wait_grad(q):
-        all_of(grecv.at[pl.ds(2 * q, 2)], g_r.at[q])
+        all_of(gedge.at[1, q], g_r.at[q])
 
     def conv(q):
         wait_grad(q)
+        gpack[...] = gedge[1, q].astype(F32) * not_last
+        for h in range(2):
+            for i in range(3):
+                gf[2 * q + h, i, ROWS : ROWS + EDGE, :] = gpack[six(h, i), :]
 
         def one(l, _):
             for i in range(3):
-                gf[l, i, ROWS : ROWS + 8, :] = grecv[l, i].astype(F32)[0:8] * not_last
                 c = tap(l, i)
                 for r in range(0, ROWS, 16):
                     total = c[0] * gf[l, i, r : r + 16, :]
@@ -472,7 +503,9 @@
 
         lax.fori_loop(2 * q, 2 * q + 2, one, 0)
 
+    gpack[6 * EDGE :, :] = jnp.zeros((48 - 6 * EDGE, 128), F32)
     tails()
+    packs()
     send_first()
     all_of(gob, ld_sem.at[2])
     order = list(range(chunks // 2, chunks)) + list(range(chunks // 2))
@@ -483,7 +516,9 @@
     c_long.wait()
     c_fwd.wait()
     spectrum()
-    all_of(raw, raw_r.at[0])
+    all_of(packb.at[1], pack_r)
+    all_of(raw, raw_r)
+    unpack()
     for l in range(tiles):
         edges(l)
     for q in range(chunks):
@@ -491,9 +526,8 @@
     for q in range(chunks // 2):
         add_x(q)
         corr(q, q == 0)
-    for q in range(chunks // 2, chunks):
-        add_y(q)
-        corr(q, False)
+        add_y(q + chunks // 2)
+        corr(q + chunks // 2, False)
     c_inv.wait()
     lags()
     gl_zero()
@@ -517,35 +551,48 @@
     gs_one(0)
     chunk(3)
     gs_zero(1)
-    gl_two()
     conv(0)
     gs_one(1)
+    conv(1)
+    conv(2)
+    gl_two(0)
+    gl_two(1)
     gs_two(0)
-    conv(1)
+    conv(3)
+    gs_two(1)
     gl_three()
-    gs_two(1)
-    conv(2)
     gs_three(0)
-    conv(3)
     gs_three(1)
     gs_four(0)
     gl_four()
     gs_four(1)
 
     all_of(raw, raw_s)
+    all_of(packb.at[0], pack_s)
     all_of(xhalo, x_s)
     all_of(yhalo.at[:, 16:TAPS, :], y_s)
-    all_of(grecv, g_s)
-    all_of(glrecv, gl_s.at[0])
+    all_of(gedge.at[0], g_s)
+    all_of(glrecv.at[0 : n_own - 1], gl_s.at[0])
     for k in range(2):
-        all_of(glex.at[k, 0 : len(rings[k][0])], gl_s.at[1 + k])
-        all_of(glex2.at[k, 0 : len(rings[k][1])], gl_s.at[3 + k])
-    all_of(glrecv, gl_s.at[5])
+        all_of(glex.at[k, 0 : counts[k][0] - 1], gl_s.at[1 + k])
+        all_of(glex2.at[k, 0 : counts[k][1] - 1], gl_s.at[3 + k])
+    all_of(glrecv.at[0 : n_own - 1], gl_s.at[5])
     for h in range(halves):
         all_of(gscore.at[h], gs_s.at[h, 0])
-        all_of(gsex.at[h, 0 : len(rings[h % 2][0])], gs_s.at[h, 1])
-        all_of(gsex2.at[h, 0 : len(rings[h % 2][1])], gs_s.at[h, 2])
-        all_of(gscore.at[h], gs_s.at[h, 3])
+        for k in range(2):
+            rows = part_rows(h, k)
+            all_of(gsex.at[h, 0 : counts[k][0] - 1, rows, :], gs_s.at[h, 1 + k])
+            all_of(gsex2.at[h, 0 : counts[k][1] - 1, rows, :], gs_s.at[h, 3 + k])
+        all_of(gscore.at[h], gs_s.at[h, 5])
+
+
+def emit(*refs):
+    sem = refs[-1]
+    copies = [pltpu.make_async_copy(refs[i], refs[3 + i], sem.at[i]) for i in range(3)]
+    for c in copies:
+        c.start()
+    for c in copies:
+        c.wait()
 
 
 def solution(mesh):
@@ -564,7 +611,7 @@
         vmem = pl.BlockSpec(memory_space=pltpu.VMEM)
         V = pltpu.VMEM
         D = pltpu.SemaphoreType.DMA
-        grad_features, grad_short, grad_long = pl.pallas_call(
+        results = pl.pallas_call(
             functools.partial(kernel, (n_seq, n_ch, n_y, n_z, lanes)),
             out_shape=(
                 V((3, ROWS, lanes), BF),
@@ -588,42 +635,38 @@
                 V((chunks, ROWS, 256), BF),
                 V((chunks, TAPS, 256), BF),
                 V((chunks, TAPS, 256), BF),
-                V((5, 16, lanes), BF),
+                V((2, 16, lanes), BF),
+                V((tiles * 3 * EDGE, 128), F32),
+                V((2, tiles * 3 * EDGE, 128), BF),
                 V((tiles, 1, 24, 128), F32),
                 V((N, 256), F32),
                 V((chunks, N, 256), F32),
                 V((chunks, N, 256), F32),
                 V((N, 256), F32),
                 V((N, 512), BF),
-                V((N, 512), BF),
                 V((ROWS, 512), F32),
                 V((tiles, 3, ROWS + 8, 128), F32),
-                V((tiles, 3, 16, 128), BF),
-                V((tiles, 3, 16, 128), BF),
-                V((TAPS, 256), F32),
-                V((n_own - 1, own_rows, 256), F32),
-                V((2, own_rows, 128), BF),
-                V((2, most - 1, own_rows, 128), BF),
-                V((2, own_rows, 128), BF),
-                V((2, most - 1, own_rows, 128), BF),
-                V((TAPS, 256), F32),
+                V((48, 128), F32),
+                V((2, chunks, 48, 128), BF),
+                V((TAPS, 256), BF),
+                V((n_own, own_rows, 256), BF),
+                V((2, most, own_rows, 128), BF),
+                V((2, most, own_rows, 128), BF),
+                V((TAPS, 256), BF),
                 V((tiles, 24, 128), F32),
                 V((halves, 2, 24, 128), F32),
-                V((halves, 48, 128), BF),
-                V((halves, most - 1, 48, 128), BF),
-                V((halves, 48, 128), BF),
-                V((halves, most - 1, 48, 128), BF),
+                V((halves, most, 48, 128), BF),
+                V((halves, most, 48, 128), BF),
                 V((tiles, 24, 128), F32),
                 D((6,)),
-                D((4,)),
-                D((1,)),
+                D((7,)),
                 D((chunks,)),
                 D((chunks,)),
                 D((chunks,)),
                 D((6,)),
                 D((6,)),
-                D((halves, 4)),
-                D((halves, 4)),
+                D((halves, 6)),
+                D((halves, 6)),
             ],
             compiler_params=pltpu.CompilerParams(
                 collective_id=0, has_side_effects=True, vmem_limit_bytes=40 * 2**20
@@ -635,6 +678,14 @@
                 for a in (features, short_filter, long_filter, grad_out, jnp.asarray(forward), jnp.asarray(inverse))
             )
         )
+        grad_features, grad_short, grad_long = pl.pallas_call(
+            emit,
+            out_shape=tuple(jax.ShapeDtypeStruct(r.shape, r.dtype) for r in results),
+            in_specs=[vmem] * 3,
+            out_specs=(pl.BlockSpec(memory_space=pl.ANY),) * 3,
+            scratch_shapes=[D((3,))],
+            name="emit",
+        )(*(pltpu.with_memory_space_constraint(r, pltpu.VMEM) for r in results))
         return grad_features, grad_short, grad_long
 
     return jax.shard_map(

time: 48.4 us -> 41.7 us (0.86)
  Pallas kernels: 45.2 us -> 40.9 us
  local copies, waits for them, and re-layouts: 2.44 us -> 0 us
    pallas_call x1, Pallas kernels: 45.2 us -> 39.7 us  [body(): pl.pallas_call(functools.partial(kernel, (n_seq, n_ch, n_y, n_z, lanes)),...]
    unnamed x3 -> x0, local copies, waits for them, and re-layouts: 2.44 us -> none
    pallas_call x0 -> x1, Pallas kernels: none -> 1.23 us  [body(): pl.pallas_call(emit, out_shape=tuple((jax.ShapeDtypeStruct(r.shape, r.dty...]
where the time goes in v3:
time: 41.7 us; the launch traced here: 41.6 us
  Pallas kernels  40.9 us (98%)
  between operations  0.64 us (2%)
    pallas_call x1, Pallas kernels, body(): pl.pallas_call(functools.partial(kernel, (n_seq, n_ch, n_y, n_z, lanes)),...  39.7 us
    pallas_call x1, Pallas kernels, body(): pl.pallas_call(emit, out_shape=tuple((jax.ShapeDtypeStruct(r.shape, r.dty...  1.23 us

profile of v3, /device:TPU:1, one launch (start us, length us, event | category | flops | bytes accessed | tf_op | source)
XLA Modules:
  0.0 41.6 jit_solution(11684956015132816661)
XLA Ops:
  0.6 39.7 %hyena_backward.1 = (bf16[3,256,1024]{2,1,0:T(8,128)(2,1)S(1)}, f32[3,7,1024]{2,1,0:T(8,128)S(1)}, f32[256,128]{1,0:T(8,128)S(1)}) custom-call(bf16[3,256,1024]{2,1,0:T(8,128)(2,1)} %feat.1, bf16[3,7,1024]{2,1,0:T(8,128)(2,1)} %short.1, bf16[256,128]{1,0:T(8,128)(2,1)} %long.1, bf16[256,1024]{1,0:T(8,128)(2,1)} %gout.1, bf16[384,768]{1,0:T(8,128)(2,1)} %constant.4.clone.fwd, ...), custom_call_target="tpu_custom_call" | custom-call | tf_op jit(solution)/shard_map/hyena_backward/pallas_call | solution.py:614
  40.3 1.2 %emit.1 = (bf16[3,256,1024]{2,1,0:T(8,128)(2,1)}, f32[3,7,1024]{2,1,0:T(8,128)}, f32[256,128]{1,0:T(8,128)}) custom-call(bf16[3,256,1024]{2,1,0:T(8,128)(2,1)S(1)} %get-tuple-element.6.refs_0_, f32[3,7,1024]{2,1,0:T(8,128)S(1)} %get-tuple-element.7.refs_1_, f32[256,128]{1,0:T(8,128)S(1)} %get-tuple-element.8.refs_2_), custom_call_target="tpu_custom_call" | custom-call | tf_op jit(solution)/shard_map/emit/pallas_call | solution.py:681

commit v4 on v3

--- a/solution.py
+++ b/solution.py
@@ -17,6 +17,7 @@
 TAPS = 128
 SHORT = 7
 EDGE = SHORT - 1
+LATE = 112
 GROUPS = 256
 N = ROWS + TAPS
 HALF = N // 2
@@ -37,7 +38,9 @@
 
     local = rows(np.arange(ROWS))
     behind = rows(np.arange(-TAPS, 0))
-    forward = np.concatenate([*split(local), *split(behind)], axis=1)
+    edge = np.concatenate([part[:, :16] for part in split(local)], axis=1)
+    blank = np.zeros((N, 96), ml_dtypes.bfloat16)
+    forward = np.concatenate([*split(local), *split(behind), edge, blank], axis=1)
     inverse = np.concatenate(split(local.T / HALF), axis=1)
     return forward, inverse
 
@@ -65,6 +68,7 @@
     vb,
     prod,
     gfil,
+    ends,
     xhalo,
     yhalo,
     raw,
@@ -92,6 +96,7 @@
     gsfin,
     ld_sem,
     halo_s,
+    halo_r,
     x_r,
     y_r,
     g_r,
@@ -147,9 +152,11 @@
 
     c_short = load(short, shortv, 0)
     for l in range(tiles):
-        load(feat.at[:, :, l * 128 : (l + 1) * 128], fb.at[l], 1)
+        load(feat.at[:, LATE:, l * 128 : (l + 1) * 128], fb.at[l, :, LATE:, :], 1)
     for l in range(tiles):
         load(gout.at[:, l * 128 : (l + 1) * 128], gob.at[l], 2)
+    for l in range(tiles):
+        load(feat.at[:, :LATE, l * 128 : (l + 1) * 128], fb.at[l, :, :LATE, :], 6)
     c_long = load(long, longv, 3)
     c_fwd = load(fwd, fwdv, 4)
     c_inv = load(inv, invv, 5)
@@ -164,7 +171,6 @@
         taps = shortv[i].astype(F32)
         for l in range(tiles):
             coef[l, i, 0:SHORT, :] = taps[:, l * 128 : (l + 1) * 128]
-    all_of(fb, ld_sem.at[1])
 
     def tap(l, i):
         return [coef[l, i, j : j + 1, :] for j in range(SHORT)]
@@ -183,36 +189,53 @@
         return pl.ds(pl.multiple_of(l * 128, 128), 128)
 
     def lane(l):
+        if isinstance(l, int):
+            return slice((l % 2) * 128, (l % 2) * 128 + 128)
         return pl.ds(pl.multiple_of(lax.rem(l, 2) * 128, 128), 128)
 
-    def product_rows(l, lo, hi):
+    def product_rows(l, lo, hi, near=False):
         ck, cv = tap(l, 1), tap(l, 2)
         for r in range(lo, hi, 16):
             k = fir(xf, l, 1, ck, 8 + r)
             v = fir(xf, l, 2, cv, 8 + r)
             kb[l, r : r + 16, :] = k
             vb[l, r : r + 16, :] = v
-            prod[l // 2, r : r + 16, lane(l)] = (k.astype(F32) * v.astype(F32)).astype(BF)
-
-    def grad_rows(l, lo, hi):
+            p = (k.astype(F32) * v.astype(F32)).astype(BF)
+            if near:
+                ends[l // 2, 0:16, lane(l)] = p
+                ends[l // 2, 16:32, lane(l)] = p
+            else:
+                prod[l // 2, r : r + 16, lane(l)] = p
+
+    def grad_rows(l, lo, hi, near=False):
         cq = tap(l, 0)
         for r in range(lo, hi, 16):
             q = fir(xf, l, 0, cq, 8 + r)
-            gfil[l // 2, r : r + 16, lane(l)] = (
-                q.astype(F32) * gob[l, r : r + 16, :].astype(F32)
-            ).astype(BF)
+            g = (q.astype(F32) * gob[l, r : r + 16, :].astype(F32)).astype(BF)
+            if near:
+                c = (l % 2) * 128 + 256
+                ends[l // 2, 0:16, c : c + 128] = g
+                ends[l // 2, 16:32, c : c + 128] = g
+            else:
+                gfil[l // 2, r : r + 16, lane(l)] = g
+
+    def lasts():
+        for l in range(tiles):
+            for i in range(3):
+                widen(l, i, ROWS - 16, ROWS)
 
     def tail(l, _):
-        widen(l, 0, ROWS - 16, ROWS)
-        widen(l, 1, 112, ROWS)
-        widen(l, 2, 112, ROWS)
+        widen(l, 1, LATE, ROWS - 16)
+        widen(l, 2, LATE, ROWS - 16)
         product_rows(l, 128, ROWS)
         return 0
 
-    def tails():
-        lax.fori_loop(0, tiles, tail, 0)
-
-    raw_s, pack_s, x_s, y_s, g_s, raw_r, pack_r = (halo_s.at[k] for k in range(7))
+    def tails(q):
+        lax.fori_loop(2 * q, 2 * q + 2, tail, 0)
+
+    raw_s = x_s = y_s = g_s = halo_s.at[0]
+    pack_s = halo_s.at[1]
+    raw_r, pack_r = halo_r.at[0], halo_r.at[1]
 
     def six(l, i):
         return slice((3 * l + i) * EDGE, (3 * l + i + 1) * EDGE)
@@ -228,8 +251,9 @@
         remote(packb.at[0], packb.at[1], pack_s, pack_r, ahead)
         remote(feat.at[0, 0:16, :], raw.at[0], raw_s, raw_r, behind)
         remote(gout.at[0:16, :], raw.at[1], raw_s, raw_r, behind)
-        for q in range(chunks):
-            remote(prod.at[q, ROWS - TAPS :, :], xhalo.at[q], x_s, x_r.at[q], ahead)
+
+    def send_tail(q):
+        remote(prod.at[q, ROWS - TAPS :, :], xhalo.at[q], x_s, x_r.at[q], ahead)
 
     def head(l, _):
         widen(l, 0, 0, 128)
@@ -242,16 +266,12 @@
     def send_head(q):
         remote(gfil.at[q, 16:TAPS, :], yhalo.at[q, 16:TAPS, :], y_s, y_r.at[q], behind)
 
-    def rest(l, _):
-        widen(l, 0, 128, ROWS)
+    def rest(l):
+        widen(l, 0, 128, ROWS - 16)
         grad_rows(l, 128, ROWS)
-        widen(l, 1, 0, 112)
-        widen(l, 2, 0, 112)
+        widen(l, 1, 0, LATE)
+        widen(l, 2, 0, LATE)
         product_rows(l, 16, 128)
-        return 0
-
-    def rests():
-        lax.fori_loop(0, tiles, rest, 0)
 
     nt = (((1,), (1,)), ((), ()))
 
@@ -271,8 +291,8 @@
             xf[l, i, 8 - EDGE : 8, :] = packf[six(l, i), :]
         qn[l, 0, 0:8, :] = xf[l, 0, ROWS : ROWS + 8, :]
         qn[l, 0, 8:24, :] = raw[0, :, cols].astype(F32)
-        product_rows(l, 0, 16)
-        grad_rows(l, 0, 16)
+        product_rows(l, 0, 16, near=True)
+        grad_rows(l, 0, 16, near=True)
         qq = fir(qn, l, 0, tap(l, 0), 8)
         yhalo[l // 2, 0:16, (l % 2) * 128 : (l % 2) * 128 + 128] = (
             qq.astype(F32) * raw[1, :, cols].astype(F32)
@@ -289,7 +309,7 @@
 
 
     def far(h):
-        return dot(fwdv[:, 2 * ROWS : 2 * ROWS + TAPS], h) + dot(fwdv[:, 2 * ROWS + TAPS :], h)
+        return dot(fwdv[:, 2 * ROWS : 2 * ROWS + TAPS], h) + dot(fwdv[:, 2 * ROWS + TAPS : 2 * N], h)
 
     def wait_x(q):
         all_of(xhalo.at[q], x_r.at[q])
@@ -304,6 +324,20 @@
     def add_y(q):
         wait_y(q)
         ys[q] = ys[q] - not_last * far(yhalo[q])
+
+    def both(halo, sign, near):
+        h = (halo.astype(F32) * sign).astype(BF)
+        return dot(fwdv[:, 2 * ROWS :], jnp.concatenate([h, h, near], axis=0))
+
+    def add_ends(q):
+        if q < chunks // 2:
+            wait_x(q)
+            xs[q] = xs[q] + both(xhalo[q], not_first, ends[q, :, 0:256])
+            ys[q] = ys[q] + dot(fwdv[:, 2 * N :], ends[q, :, 256:512])
+        else:
+            wait_y(q)
+            ys[q] = ys[q] + both(yhalo[q], -not_last, ends[q, :, 256:512])
+            xs[q] = xs[q] + dot(fwdv[:, 2 * N :], ends[q, :, 0:256])
 
     def corr(q, first):
         def block(b, _):
@@ -319,7 +353,7 @@
             rs[im, :] = ri
             return 0
 
-        lax.fori_loop(0, HALF // 16, block, 0)
+        lax.fori_loop(0, HALF // 16, block, 0, unroll=True)
 
     def hilo(value):
         high = value.astype(BF)
@@ -356,24 +390,24 @@
     def gl_zero():
         glrecv[own] = glp[piece(own), :]
         for p, o in xc_peers:
-            remote(glp.at[piece(o), :], glrecv.at[own], gl_s.at[0], gl_r.at[0], p)
+            remote(glp.at[piece(o), :], glrecv.at[own], gl_s, gl_r.at[0], p)
 
     def gl_one():
         total = gathered(glrecv, gl_r.at[0], n_own)
         for k in range(2):
             part = total[:, k * 128 : (k + 1) * 128].astype(BF)
-            spread(glex.at[k], places[k][0], part, gl_s.at[1 + k], gl_r.at[1 + k], rings[k][0])
+            spread(glex.at[k], places[k][0], part, gl_s, gl_r.at[1 + k], rings[k][0])
 
     def gl_two(k):
         part = gathered(glex.at[k], gl_r.at[1 + k], counts[k][0]).astype(BF)
-        spread(glex2.at[k], places[k][1], part, gl_s.at[3 + k], gl_r.at[3 + k], rings[k][1])
+        spread(glex2.at[k], places[k][1], part, gl_s, gl_r.at[3 + k], rings[k][1])
 
     def gl_three():
         for k in range(2):
             total = gathered(glex2.at[k], gl_r.at[3 + k], counts[k][1]) * gl_scale
             glfin[piece(own), k * 128 : (k + 1) * 128] = total.astype(BF)
         for p, _ in xc_peers:
-            remote(glfin.at[piece(own), :], glfin.at[piece(own), :], gl_s.at[5], gl_r.at[5], p)
+            remote(glfin.at[piece(own), :], glfin.at[piece(own), :], gl_s, gl_r.at[5], p)
 
     def gl_four():
         all_of(glfin.at[0 : TAPS - own_rows], gl_r.at[5])
@@ -381,7 +415,7 @@
 
     def gs_zero(h):
         theirs = pl.ds(4 * h + 2 * (1 - core), 2)
-        remote(gsp.at[theirs], gscore.at[h], gs_s.at[h, 0], gs_r.at[h, 0], sibling)
+        remote(gsp.at[theirs], gscore.at[h], gs_s.at[h], gs_r.at[h, 0], sibling)
 
     def part_rows(h, k):
         cut = 32 if h % 2 == 0 else 16
@@ -394,14 +428,14 @@
         for k in range(2):
             rows = part_rows(h, k)
             ref = gsex.at[h, :, rows, :]
-            spread(ref, places[k][0], total[rows].astype(BF), gs_s.at[h, 1 + k], gs_r.at[h, 1 + k], rings[k][0])
+            spread(ref, places[k][0], total[rows].astype(BF), gs_s.at[h], gs_r.at[h, 1 + k], rings[k][0])
 
     def gs_two(h):
         for k in range(2):
             rows = part_rows(h, k)
             part = gathered(gsex.at[h, :, rows, :], gs_r.at[h, 1 + k], counts[k][0]).astype(BF)
             ref = gsex2.at[h, :, rows, :]
-            spread(ref, places[k][1], part, gs_s.at[h, 3 + k], gs_r.at[h, 3 + k], rings[k][1])
+            spread(ref, places[k][1], part, gs_s.at[h], gs_r.at[h, 3 + k], rings[k][1])
 
     def gs_three(h):
         parts = []
@@ -411,7 +445,7 @@
         total = jnp.concatenate(parts, axis=0) * gs_scale
         here = pl.ds(4 * h + 2 * core, 2)
         gsfin[here] = total.reshape(2, 24, 128)
-        remote(gsfin.at[here], gsfin.at[here], gs_s.at[h, 5], gs_r.at[h, 5], sibling)
+        remote(gsfin.at[here], gsfin.at[here], gs_s.at[h], gs_r.at[h, 5], sibling)
 
     def gs_four(h):
         all_of(gscore.at[h], gs_r.at[h, 5])
@@ -436,7 +470,7 @@
                 spec[rows, c : c + 256] = value.astype(BF)
             return 0
 
-        lax.fori_loop(0, HALF // 16, block, 0)
+        lax.fori_loop(0, HALF // 16, block, 0, unroll=3)
 
     def inverse():
         filt[...] = dot(invv[:, 0:N], spec[...])
@@ -503,37 +537,55 @@
 
         lax.fori_loop(2 * q, 2 * q + 2, one, 0)
 
+    for q in range(chunks):
+        prod[q, 0:16, :] = jnp.zeros((16, 256), BF)
+        gfil[q, 0:16, :] = jnp.zeros((16, 256), BF)
+        ends[q, 32:, :] = jnp.zeros((96, 512), BF)
     gpack[6 * EDGE :, :] = jnp.zeros((48 - 6 * EDGE, 128), F32)
-    tails()
+    all_of(fb.at[:, :, LATE:, :], ld_sem.at[1])
+    lasts()
     packs()
+    first, second = list(range(chunks // 2)), list(range(chunks // 2, chunks))
+    for q in first:
+        tails(q)
     send_first()
+    for q in first:
+        send_tail(q)
     all_of(gob, ld_sem.at[2])
-    order = list(range(chunks // 2, chunks)) + list(range(chunks // 2))
-    for q in order:
+    all_of(fb.at[:, :, :LATE, :], ld_sem.at[6])
+    for q in second:
         heads(q)
         send_head(q)
-    rests()
-    c_long.wait()
+    for q in second:
+        tails(q)
+        send_tail(q)
+    for q in first:
+        heads(q)
+        send_head(q)
     c_fwd.wait()
-    spectrum()
+    for q in range(chunks):
+        rest(2 * q)
+        rest(2 * q + 1)
+        local(q)
     all_of(packb.at[1], pack_r)
     all_of(raw, raw_r)
     unpack()
     for l in range(tiles):
         edges(l)
-    for q in range(chunks):
-        local(q)
     for q in range(chunks // 2):
-        add_x(q)
+        add_ends(q)
         corr(q, q == 0)
-        add_y(q + chunks // 2)
+        add_ends(q + chunks // 2)
         corr(q + chunks // 2, False)
     c_inv.wait()
     lags()
     gl_zero()
-
-    def chunk(q):
-        if q < chunks // 2:
+    c_long.wait()
+    spectrum()
+
+    def chunk(h, c):
+        q = 2 * h + c
+        if h < halves // 2:
             add_y(q)
         else:
             add_x(q)
@@ -543,22 +595,22 @@
         send_grad(q)
         sgrads(q)
 
-    chunk(0)
-    chunk(1)
+    chunk(0, 1 - core)
     gs_zero(0)
-    chunk(2)
+    chunk(0, core)
+    gs_one(0)
+    chunk(1, 1 - core)
+    gs_zero(1)
     gl_one()
-    gs_one(0)
-    chunk(3)
-    gs_zero(1)
+    chunk(1, core)
+    gs_one(1)
     conv(0)
-    gs_one(1)
     conv(1)
     conv(2)
+    conv(3)
+    gs_two(0)
     gl_two(0)
     gl_two(1)
-    gs_two(0)
-    conv(3)
     gs_two(1)
     gl_three()
     gs_three(0)
@@ -567,23 +619,25 @@
     gl_four()
     gs_four(1)
 
-    all_of(raw, raw_s)
+    def left(sem, *refs):
+        size = sum(math.prod(r.shape) * jnp.dtype(r.dtype).itemsize for r in refs)
+        lines = size // 1024
+        view = xs.at[0, 0:lines, :] if lines <= N else xs.at[0:2, 0 : lines // 2, :]
+        assert math.prod(view.shape) * 4 == size
+        all_of(view, sem)
+
     all_of(packb.at[0], pack_s)
-    all_of(xhalo, x_s)
-    all_of(yhalo.at[:, 16:TAPS, :], y_s)
-    all_of(gedge.at[0], g_s)
-    all_of(glrecv.at[0 : n_own - 1], gl_s.at[0])
+    left(halo_s.at[0], raw, xhalo, yhalo.at[:, 16:TAPS, :], gedge.at[0])
+    sent = [glrecv.at[0 : n_own - 1]] * 2
     for k in range(2):
-        all_of(glex.at[k, 0 : counts[k][0] - 1], gl_s.at[1 + k])
-        all_of(glex2.at[k, 0 : counts[k][1] - 1], gl_s.at[3 + k])
-    all_of(glrecv.at[0 : n_own - 1], gl_s.at[5])
+        sent += [glex.at[k, 0 : counts[k][0] - 1], glex2.at[k, 0 : counts[k][1] - 1]]
+    left(gl_s, *sent)
     for h in range(halves):
-        all_of(gscore.at[h], gs_s.at[h, 0])
+        sent = [gscore.at[h]] * 2
         for k in range(2):
             rows = part_rows(h, k)
-            all_of(gsex.at[h, 0 : counts[k][0] - 1, rows, :], gs_s.at[h, 1 + k])
-            all_of(gsex2.at[h, 0 : counts[k][1] - 1, rows, :], gs_s.at[h, 3 + k])
-        all_of(gscore.at[h], gs_s.at[h, 5])
+            sent += [gsex.at[h, 0 : counts[k][0] - 1, rows, :], gsex2.at[h, 0 : counts[k][1] - 1, rows, :]]
+        left(gs_s.at[h], *sent)
 
 
 def emit(*refs):
@@ -623,7 +677,7 @@
             scratch_shapes=[
                 V((tiles, 3, ROWS, 128), BF),
                 V((tiles, ROWS, 128), BF),
-                V((N, 2 * N), BF),
+                V((N, 2 * N + 128), BF),
                 V((ROWS, 2 * N), BF),
                 V((3, SHORT, lanes), BF),
                 V((GROUPS, TAPS), BF),
@@ -633,6 +687,7 @@
                 V((tiles, ROWS, 128), BF),
                 V((chunks, ROWS, 256), BF),
                 V((chunks, ROWS, 256), BF),
+                V((chunks, 128, 512), BF),
                 V((chunks, TAPS, 256), BF),
                 V((chunks, TAPS, 256), BF),
                 V((2, 16, lanes), BF),
@@ -658,14 +713,15 @@
                 V((halves, most, 48, 128), BF),
                 V((halves, most, 48, 128), BF),
                 V((tiles, 24, 128), F32),
-                D((6,)),
                 D((7,)),
+                D((2,)),
+                D((2,)),
                 D((chunks,)),
                 D((chunks,)),
                 D((chunks,)),
+                D,
                 D((6,)),
-                D((6,)),
-                D((halves, 6)),
+                D((halves,)),
                 D((halves, 6)),
             ],
             compiler_params=pltpu.CompilerParams(

time: 41.7 us -> 41.2 us (0.988)
  Pallas kernels: 40.9 us -> 40.4 us
    pallas_call x1, Pallas kernels: 39.7 us -> 39.2 us  [body(): pl.pallas_call(functools.partial(kernel, (n_seq, n_ch, n_y, n_z, lanes)),...]
where the time goes in v4:
time: 41.2 us; the launch traced here: 41.1 us
  Pallas kernels  40.4 us (98%)
  between operations  0.64 us (2%)
    pallas_call x1, Pallas kernels, body(): pl.pallas_call(functools.partial(kernel, (n_seq, n_ch, n_y, n_z, lanes)),...  39.2 us
    pallas_call x1, Pallas kernels, body(): pl.pallas_call(emit, out_shape=tuple((jax.ShapeDtypeStruct(r.shape, r.dty...  1.23 us

profile of v4, /device:TPU:1, one launch (start us, length us, event | category | flops | bytes accessed | tf_op | source)
XLA Modules:
  0.0 41.1 jit_solution(16968619208990334658)
XLA Ops:
  0.6 39.2 %hyena_backward.1 = (bf16[3,256,1024]{2,1,0:T(8,128)(2,1)S(1)}, f32[3,7,1024]{2,1,0:T(8,128)S(1)}, f32[256,128]{1,0:T(8,128)S(1)}) custom-call(bf16[3,256,1024]{2,1,0:T(8,128)(2,1)} %feat.1, bf16[3,7,1024]{2,1,0:T(8,128)(2,1)} %short.1, bf16[256,128]{1,0:T(8,128)(2,1)} %long.1, bf16[256,1024]{1,0:T(8,128)(2,1)} %gout.1, bf16[384,896]{1,0:T(8,128)(2,1)} %constant.4.clone.fwd, ...), custom_call_target="tpu_custom_call" | custom-call | tf_op jit(solution)/shard_map/hyena_backward/pallas_call | solution.py:668
  39.8 1.2 %emit.1 = (bf16[3,256,1024]{2,1,0:T(8,128)(2,1)}, f32[3,7,1024]{2,1,0:T(8,128)}, f32[256,128]{1,0:T(8,128)}) custom-call(bf16[3,256,1024]{2,1,0:T(8,128)(2,1)S(1)} %get-tuple-element.6.refs_0_, f32[3,7,1024]{2,1,0:T(8,128)S(1)} %get-tuple-element.7.refs_1_, f32[256,128]{1,0:T(8,128)S(1)} %get-tuple-element.8.refs_2_), custom_call_target="tpu_custom_call" | custom-call | tf_op jit(solution)/shard_map/emit/pallas_call | solution.py:737

commit v5 on v4

--- a/solution.py
+++ b/solution.py
@@ -133,7 +133,7 @@
     n_own = 2 * n_ch
     own = ch * 2 + core
     xc_peers = []
-    for d in range(1, n_own):
+    for d in far_first(n_own):
         o = lax.rem(own + d, n_own)
         xc_peers.append(({"seq": at(y, z, lax.rem(o, 2)), "ch": o // 2}, o))
 
@@ -373,10 +373,14 @@
     rings = ((ys_peers, zs_peers), (zs_peers, ys_peers))
     places = ((y, z), (z, y))
 
-    def spread(ref, place, value, ssem, rsem, peers):
-        ref[place] = value
-        for p in peers:
-            remote(ref.at[place], ref.at[place], ssem, rsem, p)
+    def spread(rsems, ssem, refs, values, step):
+        for k in range(2):
+            refs[k][places[k][step]] = values[k]
+        for i in range(max(n_y, n_z) - 1):
+            for k in range(2):
+                if i < len(rings[k][step]):
+                    slot = refs[k].at[places[k][step]]
+                    remote(slot, slot, ssem, rsems[k], rings[k][step][i])
 
     def gathered(ref, sem, count):
         all_of(ref.at[0 : count - 1], sem)
@@ -393,14 +397,14 @@
             remote(glp.at[piece(o), :], glrecv.at[own], gl_s, gl_r.at[0], p)
 
     def gl_one():
-        total = gathered(glrecv, gl_r.at[0], n_own)
-        for k in range(2):
-            part = total[:, k * 128 : (k + 1) * 128].astype(BF)
-            spread(glex.at[k], places[k][0], part, gl_s, gl_r.at[1 + k], rings[k][0])
-
-    def gl_two(k):
-        part = gathered(glex.at[k], gl_r.at[1 + k], counts[k][0]).astype(BF)
-        spread(glex2.at[k], places[k][1], part, gl_s, gl_r.at[3 + k], rings[k][1])
+        total = gathered(glrecv, gl_r.at[0], n_own).astype(BF)
+        sems = [gl_r.at[1 + k] for k in range(2)]
+        spread(sems, gl_s, [glex.at[k] for k in range(2)], [total[:, :128], total[:, 128:]], 0)
+
+    def gl_two():
+        parts = [gathered(glex.at[k], gl_r.at[1 + k], counts[k][0]).astype(BF) for k in range(2)]
+        sems = [gl_r.at[3 + k] for k in range(2)]
+        spread(sems, gl_s, [glex2.at[k] for k in range(2)], parts, 1)
 
     def gl_three():
         for k in range(2):
@@ -425,17 +429,17 @@
         all_of(gscore.at[h], gs_r.at[h, 0])
         total = gsp[pl.ds(4 * h + 2 * core, 2)] + gscore[h]
         total = total.reshape(48, 128)
-        for k in range(2):
-            rows = part_rows(h, k)
-            ref = gsex.at[h, :, rows, :]
-            spread(ref, places[k][0], total[rows].astype(BF), gs_s.at[h], gs_r.at[h, 1 + k], rings[k][0])
+        rows = [part_rows(h, k) for k in range(2)]
+        sems = [gs_r.at[h, 1 + k] for k in range(2)]
+        spread(sems, gs_s.at[h], [gsex.at[h, :, r, :] for r in rows], [total[r].astype(BF) for r in rows], 0)
 
     def gs_two(h):
-        for k in range(2):
-            rows = part_rows(h, k)
-            part = gathered(gsex.at[h, :, rows, :], gs_r.at[h, 1 + k], counts[k][0]).astype(BF)
-            ref = gsex2.at[h, :, rows, :]
-            spread(ref, places[k][1], part, gs_s.at[h], gs_r.at[h, 3 + k], rings[k][1])
+        rows = [part_rows(h, k) for k in range(2)]
+        parts = [
+            gathered(gsex.at[h, :, rows[k], :], gs_r.at[h, 1 + k], counts[k][0]).astype(BF) for k in range(2)
+        ]
+        sems = [gs_r.at[h, 3 + k] for k in range(2)]
+        spread(sems, gs_s.at[h], [gsex2.at[h, :, r, :] for r in rows], parts, 1)
 
     def gs_three(h):
         parts = []
@@ -609,8 +613,7 @@
     conv(2)
     conv(3)
     gs_two(0)
-    gl_two(0)
-    gl_two(1)
+    gl_two()
     gs_two(1)
     gl_three()
     gs_three(0)

time: 41.2 us -> 41 us (level)
  no operation moved by 1% of the time
where the time goes in v5:
time: 41 us; the launch traced here: 40.8 us
  Pallas kernels  40.2 us (98%)
  between operations  0.64 us (2%)
    pallas_call x1, Pallas kernels, body(): pl.pallas_call(functools.partial(kernel, (n_seq, n_ch, n_y, n_z, lanes)),...  39 us
    pallas_call x1, Pallas kernels, body(): pl.pallas_call(emit, out_shape=tuple((jax.ShapeDtypeStruct(r.shape, r.dty...  1.23 us

profile of v5, /device:TPU:1, one launch (start us, length us, event | category | flops | bytes accessed | tf_op | source)
XLA Modules:
  0.0 40.8 jit_solution(7021024263869857666)
XLA Ops:
  0.6 39.0 %hyena_backward.1 = (bf16[3,256,1024]{2,1,0:T(8,128)(2,1)S(1)}, f32[3,7,1024]{2,1,0:T(8,128)S(1)}, f32[256,128]{1,0:T(8,128)S(1)}) custom-call(bf16[3,256,1024]{2,1,0:T(8,128)(2,1)} %feat.1, bf16[3,7,1024]{2,1,0:T(8,128)(2,1)} %short.1, bf16[256,128]{1,0:T(8,128)(2,1)} %long.1, bf16[256,1024]{1,0:T(8,128)(2,1)} %gout.1, bf16[384,896]{1,0:T(8,128)(2,1)} %constant.4.clone.fwd, ...), custom_call_target="tpu_custom_call" | custom-call | tf_op jit(solution)/shard_map/hyena_backward/pallas_call | solution.py:671
  39.6 1.2 %emit.1 = (bf16[3,256,1024]{2,1,0:T(8,128)(2,1)}, f32[3,7,1024]{2,1,0:T(8,128)}, f32[256,128]{1,0:T(8,128)}) custom-call(bf16[3,256,1024]{2,1,0:T(8,128)(2,1)S(1)} %get-tuple-element.6.refs_0_, f32[3,7,1024]{2,1,0:T(8,128)S(1)} %get-tuple-element.7.refs_1_, f32[256,128]{1,0:T(8,128)S(1)} %get-tuple-element.8.refs_2_), custom_call_target="tpu_custom_call" | custom-call | tf_op jit(solution)/shard_map/emit/pallas_call | solution.py:740
